TPU v7x, 128 devices: a whole 4x4x4 slice. The times are simulated.
128 devices in a mesh: section: 2 (over core), dp: 32 (over y, z_lo, x), tensor: 2 (over z_hi).
Axes of the slice: x: 4, y: 4, z: 4 (z_hi: 2, z_lo: 2; z = z_hi * 2 + z_lo), core: 2. Of those that a mesh axis runs over, the one named last changes fastest.
Arguments:
- inputs: bfloat16 [3, 32, 128, 1536], P(None, 'dp', 'tensor'), may hold values from -24 to 24
- cotangent: bfloat16 [3, 32, 128, 1536], P(None, 'dp', 'tensor'), may hold values from -6 to 6
- plan: int32 [3], replicated, may hold values from 0 to 2, each once
- attn_gain: bfloat16 [2, 1536], P('section', 'dp'), may hold values from 0.099609375 to 1.8984375
- mlp_gain: bfloat16 [2, 1536], P('section', 'dp'), may hold values from 0.099609375 to 1.8984375
- w_query: bfloat16 [2, 1536, 1536], P('section', 'dp', 'tensor'), may hold values from -0.21875 to 0.21875
- key_weight: bfloat16 [2, 1536, 768], P('section', 'dp', 'tensor'), may hold values from -0.15625 to 0.15625
- value_weight: bfloat16 [2, 1536, 768], P('section', 'dp', 'tensor'), may hold values from -0.15625 to 0.15625
- w_out: bfloat16 [2, 1536, 1536], P('section', 'tensor', 'dp'), may hold values from -0.625 to 0.625
- w_gate: bfloat16 [2, 1536, 4096], P('section', 'dp', 'tensor'), may hold values from -0.15625 to 0.15625
- w_up: bfloat16 [2, 1536, 4096], P('section', 'dp', 'tensor'), may hold values from -0.15625 to 0.15625
- w_down: bfloat16 [2, 4096, 1536], P('section', 'tensor', 'dp'), may hold values from -0.125 to 0.125
Outputs:
- layer_outputs: bfloat16 [2, 3, 32, 128, 1536], P('section', None, 'dp', 'tensor')
- input_grads: bfloat16 [2, 3, 32, 128, 1536], P('section', None, 'dp', 'tensor')
- attn_gain_grad: float32 [2, 1536], P('section', 'dp')
- mlp_gain_grad: float32 [2, 1536], P('section', 'dp')
- w_query_grad: float32 [2, 1536, 1536], P('section', 'dp', 'tensor')
- w_key_grad: float32 [2, 1536, 768], P('section', 'dp', 'tensor')
- w_value_grad: float32 [2, 1536, 768], P('section', 'dp', 'tensor')
- w_out_grad: float32 [2, 1536, 1536], P('section', 'tensor', 'dp')
- w_gate_grad: float32 [2, 1536, 4096], P('section', 'dp', 'tensor')
- w_up_grad: float32 [2, 1536, 4096], P('section', 'dp', 'tensor')
- w_down_grad: float32 [2, 4096, 1536], P('section', 'tensor', 'dp')
Inputs may be any that keep to these rules, and one draw needn't show every extreme that they name: `plan`: a permutation of the 3 micro-batches.
All inputs are finite; a program needn't handle non-finite values.
Results may differ from a plain program's by a relative error of at most 0.04.
Values may be sent and summed in bfloat16 or wider, within the bound.
No kernel may reach another device: no remote copies, remote signals or barrier semaphores. Data moves between devices by JAX's collectives and lax.ppermute only.
A program may use at most 192 MiB of HBM per device.

v0:
```python
import functools

import jax
import jax.numpy as jnp
from jax import lax
from jax.experimental import pallas as pl
from jax.experimental.pallas import tpu as pltpu
from jax.sharding import Mesh, PartitionSpec as P

HEAD_WIDTH = 96
EPSILON = 1e-05
BLOCKED = -1e30
SCORE_SCALE = HEAD_WIDTH ** (-0.5)
BF16 = jnp.bfloat16
F32 = jnp.float32

QUERY_COLS, KV_COLS = 384, 192
QKV_COLS = QUERY_COLS + 2 * KV_COLS
OUT_COLS = 384
HIDDEN_COLS = 1024
ATTN_COLS = QKV_COLS + OUT_COLS
MLP_COLS = 3 * HIDDEN_COLS
LAYER_COLS = MLP_COLS + ATTN_COLS
REST_COLS = LAYER_COLS + ATTN_COLS
HIDDEN_TILE = 512
AHEAD = 3
WIDTH = 1536
HALF = WIDTH // 2
PARTS = 2
MIB = 1024 * 1024


def swap(value, axis):
    return lax.ppermute(value, axis, [(0, 1), (1, 0)])


def pick(index, first, second):
    return jnp.where(index == 0, first, second)


def norm_back(weighted, residual, inverse):
    scaled = residual * inverse
    return inverse * (weighted - scaled * jnp.mean(weighted * scaled, axis=-1, keepdims=True))


def vmem_whole():
    return pl.BlockSpec(memory_space=pltpu.VMEM)


def smem_whole():
    return pl.BlockSpec(memory_space=pltpu.SMEM)


def shape(rows, columns, dtype):
    return jax.ShapeDtypeStruct((rows, columns), dtype)


def half_of(core_ref, which):
    position = core_ref[0] if which == 0 else 1 - core_ref[0]
    return pl.ds(pl.multiple_of(position * HALF, HALF), HALF)


def nt_dot(left_side, right_side):
    return lax.dot_general(
        left_side, right_side, (((1,), (1,)), ((), ())), preferred_element_type=F32
    )


def tn_dot(left_side, right_side):
    return lax.dot_general(
        left_side, right_side, (((0,), (0,)), ((), ())), preferred_element_type=F32
    )


def nn_dot(left_side, right_side):
    return jnp.dot(left_side, right_side, preferred_element_type=F32)


def row_parts(rows):
    return [slice(rows // PARTS * part, rows // PARTS * (part + 1)) for part in range(PARTS)]


def part_shapes(rows):
    return [shape(rows // PARTS, HALF, BF16)] * (2 * PARTS)


class Outward:
    def __init__(self, sems):
        self.sems, self.copies = sems, []

    def send(self, source, target):
        self.copies.append(pltpu.make_async_copy(source, target, self.sems.at[len(self.copies)]))
        self.copies[-1].start()

    def wait(self):
        for copy in self.copies:
            copy.wait()


def far(array):
    return pltpu.HBM(array.shape, array.dtype)


def each_sum(core_ref, sum_refs):
    rows = sum_refs[0].shape[0] * PARTS
    for which in range(2):
        for part, at in enumerate(row_parts(rows)):
            yield at, half_of(core_ref, which), sum_refs[PARTS * which + part]


def write_half(core_ref, which, left_ref, w_ref, columns, outs):
    product = nt_dot(left_ref[...], w_ref[half_of(core_ref, which), columns]).astype(BF16)
    refs = outs[PARTS * which : PARTS * (which + 1)]
    for at, ref in zip(row_parts(left_ref.shape[0]), refs):
        ref[...] = product[at]


def write_partial(core_ref, left_ref, w_ref, columns, outs):
    for which in (1, 0):
        write_half(core_ref, which, left_ref, w_ref, columns, outs)


def params(mib):
    return pltpu.CompilerParams(vmem_limit_bytes=mib * MIB)


def inverse_norm(rows):
    return lax.rsqrt(jnp.mean(rows * rows, axis=-1, keepdims=True) + EPSILON)


def causal_mask():
    row = lax.broadcasted_iota(jnp.int32, (128, 128), 0)
    return row >= lax.broadcasted_iota(jnp.int32, (128, 128), 1)


def two_heads(ref, rows, start):
    return jnp.concatenate(
        [
            ref[rows, start : start + HEAD_WIDTH],
            ref[rows, start + HEAD_WIDTH : start + 2 * HEAD_WIDTH],
        ],
        axis=0,
    )


def ahead_copy(w_any, w_ref, sem, column):
    return pltpu.make_async_copy(w_any.at[:, pl.ds(column, w_ref.shape[1])], w_ref, sem)


def attention_forward_body(sequences, core_ref, outward, first_ref, w_ref, qkv_any, prob_any, mix_ref, *rest):
    parts, (qkv_ref, prob_ref) = rest[:-2], rest[-2:]
    qkv_ref[...] = nn_dot(first_ref[...], w_ref[:, :QKV_COLS]).astype(BF16)
    outward.send(qkv_ref, qkv_any)
    mask = causal_mask()
    mask = jnp.concatenate([mask, mask], axis=0)
    for sequence in range(sequences):
        rows = slice(128 * sequence, 128 * (sequence + 1))
        for group in range(2):
            queries = two_heads(qkv_ref, rows, 2 * HEAD_WIDTH * group)
            key_at = QUERY_COLS + HEAD_WIDTH * group
            value_at = key_at + KV_COLS
            scores = nt_dot(queries, qkv_ref[rows, key_at : key_at + HEAD_WIDTH]) * SCORE_SCALE
            scores = jnp.where(mask, scores, BLOCKED)
            expanded = jnp.exp(scores - jnp.max(scores, axis=-1, keepdims=True))
            probability = expanded / jnp.sum(expanded, axis=-1, keepdims=True)
            prob_ref[2 * sequence + group] = probability
            mixed = nn_dot(
                probability.astype(BF16), qkv_ref[rows, value_at : value_at + HEAD_WIDTH]
            ).astype(BF16)
            at = 2 * HEAD_WIDTH * group
            mix_ref[rows, at : at + HEAD_WIDTH] = mixed[:128]
            mix_ref[rows, at + HEAD_WIDTH : at + 2 * HEAD_WIDTH] = mixed[128:]
        both = pl.ds(2 * sequence, 2)
        outward.send(prob_ref.at[both], prob_any.at[both])
    write_partial(core_ref, mix_ref, w_ref, slice(QKV_COLS, ATTN_COLS), parts)
    outward.wait()


def attention_first_kernel(sequences, column, core_ref, x_ref, w_any, first_any, *rest):
    outs, (first_ref, w_ref, sem, sems) = rest[:-4], rest[-4:]
    copy = ahead_copy(w_any, w_ref, sem, column)
    copy.start()
    rows = x_ref[...].astype(F32)
    first_ref[...] = (rows * inverse_norm(rows)).astype(BF16)
    copy.wait()
    outward = Outward(sems)
    outward.send(first_ref, first_any)
    attention_forward_body(sequences, core_ref, outward, first_ref, w_ref, *outs)


def attention_next_kernel(sequences, core_ref, middle_ref, *rest):
    sums, (w_ref, _, x_any, first_any) = rest[: 2 * PARTS], rest[2 * PARTS : 2 * PARTS + 4]
    outs, (x_ref, first_ref, sems) = rest[2 * PARTS + 4 : -3], rest[-3:]
    outward = Outward(sems)
    for at, columns, part in each_sum(core_ref, sums):
        x_ref[at, columns] = (middle_ref[at, columns] + part[...].astype(F32)).astype(BF16)
    outward.send(x_ref, x_any)
    rows = x_ref[...].astype(F32)
    first_ref[...] = (rows * inverse_norm(rows)).astype(BF16)
    outward.send(first_ref, first_any)
    attention_forward_body(sequences, core_ref, outward, first_ref, w_ref, *outs)


def in_hbm(value):
    return pltpu.with_memory_space_constraint(value, pltpu.HBM)


def hbm_whole():
    return pl.BlockSpec(memory_space=pltpu.HBM)


def attention_scratch():
    return [pltpu.VMEM((WIDTH, ATTN_COLS), BF16), pltpu.SemaphoreType.DMA(())]


def attention_outs(rows):
    outs = [
        shape(rows, WIDTH, BF16),
        far(shape(rows, QKV_COLS, BF16)),
        pltpu.HBM((rows // 64, 256, 128), F32),
        shape(rows, OUT_COLS, BF16),
    ]
    return outs + part_shapes(rows), [vmem_whole(), hbm_whole(), hbm_whole()] + [vmem_whole()] * (1 + 2 * PARTS)


def attention_cost(rows):
    return pl.CostEstimate(
        flops=2 * rows * WIDTH * ATTN_COLS, bytes_accessed=8_000_000, transcendentals=0
    )


def fetch_kernel(column, w_any, *rest):
    out_ref, token_ref, sem = rest[-3:]
    copy = ahead_copy(w_any, out_ref, sem, column)
    copy.start()
    token_ref[...] = jnp.zeros_like(token_ref)
    copy.wait()


TOKEN = jax.ShapeDtypeStruct((8, 128), F32)


def fetch(weights, column, columns, *after):
    return pl.pallas_call(
        functools.partial(fetch_kernel, column),
        in_specs=[hbm_whole()] * (1 + len(after)),
        out_specs=[vmem_whole()] * 2,
        out_shape=[shape(WIDTH, columns, BF16), TOKEN],
        scratch_shapes=[pltpu.SemaphoreType.DMA(())],
        compiler_params=params(12),
        cost_estimate=pl.CostEstimate(
            flops=0, bytes_accessed=2 * WIDTH * columns * 2, transcendentals=0
        ),
        name="fetch",
    )(in_hbm(weights), *[in_hbm(value) for value in after])


def attention_first(core, x, weights, column):
    rows = x.shape[0]
    outs, specs = attention_outs(rows)
    return pl.pallas_call(
        functools.partial(attention_first_kernel, rows // 128, column),
        in_specs=[smem_whole(), vmem_whole(), hbm_whole()],
        out_specs=[hbm_whole()] + specs[1:],
        out_shape=[far(outs[0])] + outs[1:],
        scratch_shapes=[
            pltpu.VMEM((rows, QKV_COLS), BF16),
            pltpu.VMEM((rows // 64, 256, 128), F32),
            pltpu.VMEM((rows, WIDTH), BF16),
        ]
        + attention_scratch()
        + [pltpu.SemaphoreType.DMA((2 + rows // 128,))],
        compiler_params=params(20),
        cost_estimate=attention_cost(rows),
        name="attention_first",
    )(core, x, in_hbm(weights))


def attention_next(core, middle, sums, weights, token):
    rows = middle.shape[0]
    outs, specs = attention_outs(rows)
    whole = shape(rows, WIDTH, BF16)
    return pl.pallas_call(
        functools.partial(attention_next_kernel, rows // 128),
        in_specs=[smem_whole()] + [vmem_whole()] * (2 + 2 * PARTS) + [hbm_whole()],
        out_specs=[hbm_whole()] * 2 + specs[1:],
        out_shape=[far(whole)] * 2 + outs[1:],
        scratch_shapes=[
            pltpu.VMEM((rows, QKV_COLS), BF16),
            pltpu.VMEM((rows // 64, 256, 128), F32),
            pltpu.VMEM(whole.shape, BF16),
            pltpu.VMEM(whole.shape, BF16),
            pltpu.SemaphoreType.DMA((3 + rows // 128,)),
        ],
        compiler_params=params(16),
        cost_estimate=attention_cost(rows),
        name="attention_next",
    )(core, middle, *sums, weights, token)


def column_tiles(first):
    return [pl.ds(first + HIDDEN_TILE * step, HIDDEN_TILE) for step in range(HIDDEN_STEPS)]


def sigmoid(values):
    return 0.5 * jnp.tanh(0.5 * values) + 0.5


def arrivals(copies):
    for copy in copies[:AHEAD]:
        copy.start()
    place = iter(range(len(copies)))

    def arrive():
        number = next(place)
        copies[number].wait()
        if number + AHEAD < len(copies):
            copies[number + AHEAD].start()

    return arrive


def mlp_forward_kernel(core_ref, x_ref, *rest):
    sums, rest = rest[: 2 * PARTS], rest[2 * PARTS :]
    (w_ref, _, middle_any, second_any, gate_any, up_any, hidden_any), rest = rest[:7], rest[7:]
    outs, (middle_ref, second_ref, gate_ref, up_ref, hidden_ref, out_sems) = rest[:-6], rest[-6:]
    tiles = [(gate, up) for gate, up in zip(column_tiles(0), column_tiles(HIDDEN_COLS))]
    down = pl.ds(2 * HIDDEN_COLS, HIDDEN_COLS)
    for at, columns, part in each_sum(core_ref, sums):
        middle_ref[at, columns] = x_ref[at, columns].astype(F32) + part[...].astype(F32)
    rows = middle_ref[...]
    second_ref[...] = (rows * inverse_norm(rows)).astype(BF16)
    outward = Outward(out_sems)
    outward.send(middle_ref, middle_any)
    outward.send(second_ref, second_any)
    for step, (gate, up) in enumerate(tiles):
        at = slice(HIDDEN_TILE * step, HIDDEN_TILE * (step + 1))
        gate_out = nn_dot(second_ref[...], w_ref[:, gate])
        up_out = nn_dot(second_ref[...], w_ref[:, up])
        gate_ref[:, at] = gate_out
        up_ref[:, at] = up_out
        hidden_ref[:, at] = (gate_out * sigmoid(gate_out) * up_out).astype(BF16)
        for ref, target in ((gate_ref, gate_any), (up_ref, up_any), (hidden_ref, hidden_any)):
            outward.send(ref.at[:, at], target.at[:, at])
    write_partial(core_ref, hidden_ref, w_ref, down, outs)
    outward.wait()


HIDDEN_STEPS = HIDDEN_COLS // HIDDEN_TILE


def mlp_cost(rows):
    return pl.CostEstimate(
        flops=2 * rows * WIDTH * MLP_COLS, bytes_accessed=15_000_000, transcendentals=0
    )


def mlp_forward(core, x, sums, weights, token):
    rows = x.shape[0]
    saved = [
        shape(rows, WIDTH, F32),
        shape(rows, WIDTH, BF16),
        shape(rows, HIDDEN_COLS, F32),
        shape(rows, HIDDEN_COLS, F32),
        shape(rows, HIDDEN_COLS, BF16),
    ]
    return pl.pallas_call(
        mlp_forward_kernel,
        in_specs=[smem_whole()] + [vmem_whole()] * (2 + 2 * PARTS) + [hbm_whole()],
        out_specs=[hbm_whole()] * 5 + [vmem_whole()] * (2 * PARTS),
        out_shape=[far(array) for array in saved] + part_shapes(rows),
        scratch_shapes=[pltpu.VMEM(out.shape, out.dtype) for out in saved]
        + [pltpu.SemaphoreType.DMA((2 + 3 * HIDDEN_STEPS,))],
        compiler_params=params(24),
        cost_estimate=mlp_cost(rows),
        name="mlp_forward",
    )(core, x, *sums, weights, token)


def mlp_grads(hidden_grad, gate_out, up_out):
    sigmoid_gate = sigmoid(gate_out)
    gate_grad = hidden_grad * up_out * (sigmoid_gate * (1.0 + gate_out * (1.0 - sigmoid_gate)))
    return gate_grad.astype(BF16), (hidden_grad * (gate_out * sigmoid_gate)).astype(BF16)


def mlp_backward_kernel(core_ref, x_ref, middle_grad_ref, *rest):
    sums, rest = rest[: 2 * PARTS], rest[2 * PARTS :]
    (gate_ref, up_ref, w_ref, _, g_ref, pair_grad_ref), rest = rest[:6], rest[6:]
    outs, weighted = rest[:-1], rest[-1]
    for at, columns, part in each_sum(core_ref, sums):
        weighted[at, columns] = part[...].astype(F32)
    rows = x_ref[...].astype(F32)
    g_ref[...] = (
        middle_grad_ref[...] + norm_back(weighted[...], rows, inverse_norm(rows))
    ).astype(BF16)
    for step, down in enumerate(column_tiles(2 * HIDDEN_COLS)):
        at = slice(HIDDEN_TILE * step, HIDDEN_TILE * (step + 1))
        up_at = slice(HIDDEN_COLS + at.start, HIDDEN_COLS + at.stop)
        hidden_grad = nn_dot(g_ref[...], w_ref[:, down])
        pair_grad_ref[:, at], pair_grad_ref[:, up_at] = mlp_grads(
            hidden_grad, gate_ref[:, at], up_ref[:, at]
        )
    write_partial(core_ref, pair_grad_ref, w_ref, slice(0, 2 * HIDDEN_COLS), outs)


def mlp_backward(core, above, gate_out, up_out, weights, token):
    rows = gate_out.shape[0]
    return pl.pallas_call(
        mlp_backward_kernel,
        in_specs=[smem_whole()] + [vmem_whole()] * (5 + 2 * PARTS) + [hbm_whole()],
        out_specs=[vmem_whole()] * (2 + 2 * PARTS),
        out_shape=[shape(rows, WIDTH, BF16), shape(rows, 2 * HIDDEN_COLS, BF16)]
        + part_shapes(rows),
        scratch_shapes=[pltpu.VMEM((rows, WIDTH), F32)],
        compiler_params=params(26),
        cost_estimate=mlp_cost(rows),
        name="mlp_backward",
    )(core, *above, gate_out, up_out, weights, token)


def mlp_ahead_kernel(g_ref, w_any, hidden_grad_ref, pair_ref, token_ref, down_ref, sems):
    down = ahead_copy(w_any, down_ref, sems.at[0], 2 * HIDDEN_COLS)
    pair = ahead_copy(w_any, pair_ref, sems.at[1], 0)
    down.start()
    pair.start()
    token_ref[...] = jnp.zeros_like(token_ref)
    down.wait()
    hidden_grad_ref[...] = nn_dot(g_ref[...], down_ref[...])
    pair.wait()


def mlp_ahead(g, weights):
    rows = g.shape[0]
    return pl.pallas_call(
        mlp_ahead_kernel,
        in_specs=[vmem_whole(), hbm_whole()],
        out_specs=[vmem_whole()] * 3,
        out_shape=[
            shape(rows, HIDDEN_COLS, F32),
            shape(WIDTH, 2 * HIDDEN_COLS, BF16),
            TOKEN,
        ],
        scratch_shapes=[pltpu.VMEM((WIDTH, HIDDEN_COLS), BF16), pltpu.SemaphoreType.DMA((2,))],
        compiler_params=params(15),
        cost_estimate=pl.CostEstimate(
            flops=2 * rows * WIDTH * HIDDEN_COLS, bytes_accessed=14_000_000, transcendentals=0
        ),
        name="mlp_ahead",
    )(g, in_hbm(weights))


def mlp_last_kernel(core_ref, x_ref, *rest):
    sums, rest = rest[: 2 * PARTS], rest[2 * PARTS :]
    (hidden_grad_ref, w_ref, _, middle_any, hidden_any, second_ref, hidden_ref, pair_grad_ref), rest = rest[:8], rest[8:]
    middle_ref, out_sems = rest
    for at, columns, part in each_sum(core_ref, sums):
        middle_ref[at, columns] = x_ref[at, columns].astype(F32) + part[...].astype(F32)
    rows = middle_ref[...]
    second_ref[...] = (rows * inverse_norm(rows)).astype(BF16)
    outward = Outward(out_sems)
    outward.send(middle_ref, middle_any)
    for step, (gate, up) in enumerate(zip(column_tiles(0), column_tiles(HIDDEN_COLS))):
        at = slice(HIDDEN_TILE * step, HIDDEN_TILE * (step + 1))
        up_at = slice(HIDDEN_COLS + at.start, HIDDEN_COLS + at.stop)
        gate_out = nn_dot(second_ref[...], w_ref[:, gate])
        up_out = nn_dot(second_ref[...], w_ref[:, up])
        hidden_ref[:, at] = (gate_out * sigmoid(gate_out) * up_out).astype(BF16)
        pair_grad_ref[:, at], pair_grad_ref[:, up_at] = mlp_grads(
            hidden_grad_ref[:, at], gate_out, up_out
        )
    outward.send(hidden_ref, hidden_any)
    outward.wait()


def mlp_last(core, x, sums, hidden_grad, pair_weights, token):
    rows = x.shape[0]
    return pl.pallas_call(
        mlp_last_kernel,
        in_specs=[smem_whole()] + [vmem_whole()] * (3 + 2 * PARTS) + [hbm_whole()],
        out_specs=[hbm_whole()] * 2 + [vmem_whole()] * 3,
        out_shape=[
            pltpu.HBM((rows, WIDTH), F32),
            pltpu.HBM((rows, HIDDEN_COLS), BF16),
            shape(rows, WIDTH, BF16),
            shape(rows, HIDDEN_COLS, BF16),
            shape(rows, 2 * HIDDEN_COLS, BF16),
        ],
        scratch_shapes=[pltpu.VMEM((rows, WIDTH), F32), pltpu.SemaphoreType.DMA((2,))],
        compiler_params=params(28),
        cost_estimate=mlp_cost(rows),
        name="mlp_last",
    )(core, x, *sums, hidden_grad, pair_weights, token)


def mlp_in_kernel(core_ref, pair_grad_ref, w_any, _, *rest):
    outs, w_ref, sems = rest[:-2], rest[-2], rest[-1]
    copies = []
    for which in (1, 0):
        half = half_of(core_ref, which)
        source = w_any.at[half, pl.ds(0, 2 * HIDDEN_COLS)]
        copies.append(pltpu.make_async_copy(source, w_ref.at[half, :], sems.at[which]))
        copies[-1].start()
    for copy, which in zip(copies, (1, 0)):
        copy.wait()
        write_half(core_ref, which, pair_grad_ref, w_ref, slice(0, 2 * HIDDEN_COLS), outs)


def mlp_in(core, pair_grad, weights, token):
    rows = pair_grad.shape[0]
    return pl.pallas_call(
        mlp_in_kernel,
        in_specs=[smem_whole(), vmem_whole()] + [hbm_whole()] * 2,
        out_specs=[vmem_whole()] * (2 * PARTS),
        out_shape=part_shapes(rows),
        scratch_shapes=[
            pltpu.VMEM((WIDTH, 2 * HIDDEN_COLS), BF16),
            pltpu.SemaphoreType.DMA((2,)),
        ],
        compiler_params=params(18),
        cost_estimate=pl.CostEstimate(
            flops=4 * rows * WIDTH * HIDDEN_COLS, bytes_accessed=9_000_000, transcendentals=0
        ),
        name="mlp_in",
    )(core, pair_grad, in_hbm(weights), token)


def mlp_down_kernel(core_ref, hidden_ref, w_any, *rest):
    outs, w_ref, sem = rest[:-2], rest[-2], rest[-1]
    copy = pltpu.make_async_copy(w_any.at[:, pl.ds(2 * HIDDEN_COLS, HIDDEN_COLS)], w_ref, sem)
    copy.start()
    copy.wait()
    write_partial(core_ref, hidden_ref, w_ref, slice(0, HIDDEN_COLS), outs)


def mlp_down(core, hidden, weights):
    rows = hidden.shape[0]
    return pl.pallas_call(
        mlp_down_kernel,
        in_specs=[smem_whole(), vmem_whole(), hbm_whole()],
        out_specs=[vmem_whole()] * (2 * PARTS),
        out_shape=part_shapes(rows),
        scratch_shapes=[pltpu.VMEM((WIDTH, HIDDEN_COLS), BF16), pltpu.SemaphoreType.DMA(())],
        compiler_params=params(14),
        cost_estimate=pl.CostEstimate(
            flops=2 * rows * WIDTH * HIDDEN_COLS, bytes_accessed=5_000_000, transcendentals=0
        ),
        name="mlp_down",
    )(core, hidden, in_hbm(weights))


def attention_backward_kernel(sequences, near, core_ref, g_ref, middle_ref, *rest):
    sums, rest = rest[: 2 * PARTS], rest[2 * PARTS :]
    (w_ref, qkv_any, prob_any, _, middle_grad_out, attn_in_ref, qkv_grad_ref), rest = rest[:7], rest[7:]
    outs, (middle_grad_ref, qkv_ref, prob_ref, mix_grad, sems) = rest[:-5], rest[-5:]
    copies = [
        pltpu.make_async_copy(qkv_any, qkv_ref, sems.at[0]),
        pltpu.make_async_copy(prob_any, prob_ref, sems.at[1]),
    ]
    for copy in copies:
        copy.start()
    for at, columns, part in each_sum(core_ref, sums):
        middle_grad_ref[at, columns] = part[...].astype(F32)
    middle = middle_ref[...]
    middle_grad = g_ref[...].astype(F32) + norm_back(
        middle_grad_ref[...], middle, inverse_norm(middle)
    )
    if near:
        middle_grad_out[...] = middle_grad
    else:
        middle_grad_ref[...] = middle_grad
        outward = pltpu.make_async_copy(middle_grad_ref, middle_grad_out, sems.at[2])
        outward.start()
    attn_in_ref[...] = middle_grad.astype(BF16)
    mix_grad[...] = nn_dot(attn_in_ref[...], w_ref[:, QKV_COLS:]).astype(BF16)
    for copy in copies:
        copy.wait()
    for sequence in range(sequences):
        rows = slice(128 * sequence, 128 * (sequence + 1))
        for group in range(2):
            at = 2 * HEAD_WIDTH * group
            key_at = QUERY_COLS + HEAD_WIDTH * group
            value_at = key_at + KV_COLS
            grads = two_heads(mix_grad, rows, at)
            queries = two_heads(qkv_ref, rows, at)
            keys = qkv_ref[rows, key_at : key_at + HEAD_WIDTH]
            probability = prob_ref[2 * sequence + group]
            prob_grad = nt_dot(grads, qkv_ref[rows, value_at : value_at + HEAD_WIDTH])
            centred = jnp.sum(probability * prob_grad, axis=-1, keepdims=True)
            score_grad = (probability * (prob_grad - centred)).astype(BF16)
            query_grad = (nn_dot(score_grad, keys) * SCORE_SCALE).astype(BF16)
            qkv_grad_ref[rows, at : at + HEAD_WIDTH] = query_grad[:128]
            qkv_grad_ref[rows, at + HEAD_WIDTH : at + 2 * HEAD_WIDTH] = query_grad[128:]
            qkv_grad_ref[rows, key_at : key_at + HEAD_WIDTH] = (
                tn_dot(score_grad, queries) * SCORE_SCALE
            ).astype(BF16)
            qkv_grad_ref[rows, value_at : value_at + HEAD_WIDTH] = tn_dot(
                probability.astype(BF16), grads
            ).astype(BF16)
    if near:
        write_partial(core_ref, qkv_grad_ref, w_ref, slice(0, QKV_COLS), outs)
    else:
        outward.wait()


def attention_in_kernel(core_ref, qkv_grad_ref, w_ref, _, *outs):
    write_partial(core_ref, qkv_grad_ref, w_ref, slice(0, QKV_COLS), outs)


def attention_in(core, qkv_grad, weights, token):
    rows = qkv_grad.shape[0]
    return pl.pallas_call(
        attention_in_kernel,
        in_specs=[smem_whole()] + [vmem_whole()] * 2 + [hbm_whole()],
        out_specs=[vmem_whole()] * (2 * PARTS),
        out_shape=part_shapes(rows),
        compiler_params=params(14),
        cost_estimate=pl.CostEstimate(
            flops=2 * rows * WIDTH * QKV_COLS, bytes_accessed=5_000_000, transcendentals=0
        ),
        name="attention_in",
    )(core, qkv_grad, weights, token)


def attention_backward(core, g, middle, sums, qkv, probability, weights, token, near):
    rows = g.shape[0]
    residual, parts = shape(rows, WIDTH, F32), part_shapes(rows) if near else []
    return pl.pallas_call(
        functools.partial(attention_backward_kernel, rows // 128, near),
        in_specs=[smem_whole()] + [vmem_whole()] * (3 + 2 * PARTS) + [hbm_whole()] * 3,
        out_specs=[vmem_whole() if near else hbm_whole()] + [vmem_whole()] * (2 + len(parts)),
        out_shape=[
            residual if near else far(residual),
            shape(rows, WIDTH, BF16),
            shape(rows, QKV_COLS, BF16),
        ]
        + parts,
        scratch_shapes=[
            pltpu.VMEM((rows, WIDTH), F32),
            pltpu.VMEM(qkv.shape, BF16),
            pltpu.VMEM(probability.shape, F32),
            pltpu.VMEM((rows, OUT_COLS), BF16),
            pltpu.SemaphoreType.DMA((3,)),
        ],
        compiler_params=params(24),
        cost_estimate=attention_cost(rows),
        name="attention_backward",
    )(core, g, middle, *sums, weights, in_hbm(qkv), in_hbm(probability), token)


def write_products(start, pairs, out_any, slots, sems):
    _, height, width = slots.shape
    copies = []
    for number in range(WIDTH // height):
        features = pl.ds(height * number, height)
        if number >= 2:
            copies[number - 2].wait()
        slot = slots.at[number % 2]
        at = 0
        for left, right in pairs:
            columns = right.shape[1]
            slot[:, at : at + columns] = tn_dot(left[:, features], right[...]).astype(BF16)
            at += columns
        target = out_any.at[features, pl.ds(start, width)]
        copies.append(pltpu.make_async_copy(slot, target, sems.at[number % 2]))
        copies[-1].start()
    for copy in copies[-2:]:
        copy.wait()


def mlp_weights_kernel(second_ref, g_ref, pair_grad_ref, hidden_ref, *rest):
    out_any, token_ref, slots, sems = rest[-4:]
    token_ref[...] = jnp.zeros_like(token_ref)
    write_products(0, [(second_ref, pair_grad_ref), (g_ref, hidden_ref)], out_any, slots, sems)


def into_buffer(kernel, buffer, columns, slot, operands, flops, name, mib):
    aliases, specs = {}, [vmem_whole()] * len(operands)
    if buffer is not None:
        aliases = {len(operands): 0}
        specs, operands = specs + [hbm_whole()], operands + (in_hbm(buffer),)
    return pl.pallas_call(
        kernel,
        in_specs=specs,
        out_specs=[hbm_whole(), vmem_whole()],
        out_shape=[pltpu.HBM((WIDTH, columns), BF16), TOKEN],
        input_output_aliases=aliases,
        scratch_shapes=[pltpu.VMEM((2, *slot), BF16), pltpu.SemaphoreType.DMA((2,))],
        compiler_params=params(mib),
        cost_estimate=pl.CostEstimate(flops=flops, bytes_accessed=flops // 250, transcendentals=0),
        name=name,
    )(*operands)


def mlp_weights(buffer, columns, second, g, pair_grad, hidden):
    return into_buffer(
        mlp_weights_kernel,
        buffer,
        columns,
        (512, MLP_COLS),
        (second, g, pair_grad, hidden),
        2 * second.shape[0] * WIDTH * MLP_COLS,
        "mlp_weights",
        18,
    )


def attention_weights_kernel(start, first_ref, attn_in_ref, qkv_grad_ref, mix_ref, *rest):
    out_any, token_ref, slots, sems = rest[-4:]
    token_ref[...] = jnp.zeros_like(token_ref)
    pairs = [(first_ref, qkv_grad_ref), (attn_in_ref, mix_ref)]
    write_products(start, pairs, out_any, slots, sems)


def attention_weights(buffer, columns, start, first, attn_in, qkv_grad, mixture):
    return into_buffer(
        functools.partial(attention_weights_kernel, start),
        buffer,
        columns,
        (768, ATTN_COLS),
        (first, attn_in, qkv_grad, mixture),
        2 * first.shape[0] * WIDTH * ATTN_COLS,
        "attention_weights",
        14,
    )


def sum_four(partial, beside=None, within=None):
    keeps, gives = list(partial[:PARTS]), list(partial[PARTS:])
    chips = [
        (keep.astype(F32) + swap(give, "section").astype(F32)).astype(BF16)
        for keep, give in zip(keeps, gives)
    ]
    arrived = [swap(chip, "tensor") for chip in chips]
    if beside is not None:
        arrived[-1], beside = lax.optimization_barrier((arrived[-1], beside))
    totals = [
        (chip.astype(F32) + other.astype(F32)).astype(BF16)
        for chip, other in zip(chips, arrived)
    ]
    if within is not None:

        def tie(value):
            totals[0], value = lax.optimization_barrier((totals[0], value))
            return value

        beside = within(tie)
    return totals + [swap(total, "section") for total in totals], beside


def row_scales(gain_ref):
    row = lax.broadcasted_iota(jnp.int32, (48, 48), 0)
    column = lax.broadcasted_iota(jnp.int32, (48, 48), 1)
    return jnp.where(row == column, gain_ref[...].astype(F32), 0.0).astype(BF16)


def pack_kernel(core_ref, *rest):
    sources, (mine_ref, give_ref), shards, sems = rest[:9], rest[9:11], rest[11:20], rest[20]
    copies = [
        pltpu.make_async_copy(source, shard, sems.at[number])
        for number, (source, shard) in enumerate(zip(sources, shards))
    ]
    for copy in copies:
        copy.start()
    is_first = core_ref[0] == 0
    (attn_gain_ref, mlp_gain_ref), shards = shards[:2], shards[2:]
    for copy in copies[:2]:
        copy.wait()
    attn_scale, mlp_scale = row_scales(attn_gain_ref), row_scales(mlp_gain_ref)
    start = 0
    for copy, shard, scale in zip(
        copies[2:],
        shards,
        (mlp_scale, mlp_scale, None, attn_scale, attn_scale, attn_scale, None),
    ):
        copy.wait()
        weight = shard[...]
        if scale is not None:
            weight = nn_dot(scale, weight).astype(BF16)
        width = weight.shape[1] // 2
        low, high = weight[:, :width], weight[:, width:]
        mine_ref[:, start : start + width] = jnp.where(is_first, low, high)
        give_ref[:, start : start + width] = jnp.where(is_first, high, low)
        start += width


def pack_shards(core, *shards):
    return pl.pallas_call(
        pack_kernel,
        in_specs=[smem_whole()] + [hbm_whole()] * len(shards),
        out_specs=[vmem_whole()] * 2,
        out_shape=[shape(48, LAYER_COLS, BF16)] * 2,
        scratch_shapes=[pltpu.VMEM(shard.shape, shard.dtype) for shard in shards]
        + [pltpu.SemaphoreType.DMA((len(shards),))],
        compiler_params=params(16),
        name="pack_shards",
    )(core, *[in_hbm(shard) for shard in shards])


def combine_kernel(core_ref, keep_ref, arrived_ref, last_ref, zero_w_ref, one_w_ref, mine_ref, give_ref, terms_ref, zero, one):
    rest = (keep_ref[...].astype(F32) + arrived_ref[...].astype(F32)).astype(BF16)
    zero[:, :MLP_COLS] = rest[:, :MLP_COLS]
    zero[:, MLP_COLS:] = rest[:, LAYER_COLS:]
    one[:, :MLP_COLS] = last_ref[...]
    one[:, MLP_COLS:] = rest[:, MLP_COLS:LAYER_COLS]
    is_first = core_ref[0] == 0
    mine_ref[...] = jnp.where(is_first, zero[...], one[...])
    give_ref[...] = jnp.where(is_first, one[...], zero[...])
    row = 0
    for grad, weights in ((zero, zero_w_ref), (one, one_w_ref)):
        products = weights[...].astype(F32) * grad[...].astype(F32)
        for columns in (slice(MLP_COLS, MLP_COLS + QKV_COLS), slice(0, 2 * HIDDEN_COLS)):
            terms_ref[row, :] = jnp.sum(products[:, columns], axis=1)
            row += 1


def combine_grads(core, *operands):
    return pl.pallas_call(
        combine_kernel,
        in_specs=[smem_whole()] + [vmem_whole()] * len(operands),
        out_specs=[vmem_whole()] * 3,
        out_shape=[shape(48, LAYER_COLS, BF16)] * 2 + [shape(4, 48, F32)],
        scratch_shapes=[pltpu.VMEM((48, LAYER_COLS), BF16)] * 2,
        compiler_params=params(16),
        name="combine_grads",
    )(core, *operands)


def unpack_kernel(core_ref, attn_scale_ref, mlp_scale_ref, mine_ref, got_ref, gate_ref, up_ref, down_ref, query_ref, key_ref, value_ref, out_ref):
    is_first = core_ref[0] == 0

    def place(out, start, scale_ref):
        width = out.shape[1] // 2
        mine = mine_ref[:, start : start + width].astype(F32)
        got = got_ref[:, start : start + width].astype(F32)
        if scale_ref is not None:
            mine, got = mine * scale_ref[...], got * scale_ref[...]
        out[:, :width] = jnp.where(is_first, mine, got)
        out[:, width:] = jnp.where(is_first, got, mine)

    place(gate_ref, 0, mlp_scale_ref)
    place(up_ref, HIDDEN_COLS, mlp_scale_ref)
    place(down_ref, 2 * HIDDEN_COLS, None)
    place(query_ref, MLP_COLS, attn_scale_ref)
    place(key_ref, MLP_COLS + QUERY_COLS, attn_scale_ref)
    place(value_ref, MLP_COLS + QUERY_COLS + KV_COLS, attn_scale_ref)
    place(out_ref, MLP_COLS + QKV_COLS, None)


def unpack_grads(core, *operands):
    widths = [HIDDEN_COLS] * 3 + [QUERY_COLS, KV_COLS, KV_COLS, OUT_COLS]
    return pl.pallas_call(
        unpack_kernel,
        in_specs=[smem_whole()] + [vmem_whole()] * len(operands),
        out_specs=[vmem_whole()] * len(widths),
        out_shape=[shape(48, 2 * width, F32) for width in widths],
        compiler_params=params(16),
        name="unpack_grads",
    )(core, *operands)


def gather_rows(z_low, share):
    other = swap(share, "zl")
    pair = jnp.concatenate([pick(z_low, share, other), pick(z_low, other, share)], axis=0)
    return lax.all_gather(pair, ("y", "x"), axis=0, tiled=True)


def scatter_pair(grad):
    return lax.psum_scatter(grad, ("y", "x"), scatter_dimension=0, tiled=True)


def scatter_low(z_low, pair):
    keep = pick(z_low, pair[:48], pair[48:])
    give = pick(z_low, pair[48:], pair[:48])
    return (keep.astype(F32) + swap(give, "zl").astype(F32)).astype(BF16)


def to_ring_order(rows):
    lead = rows.shape[:-1]
    return jnp.swapaxes(rows.reshape(lead + (4, 2, 4, 48)), -3, -2).reshape(rows.shape)


def from_ring_order(rows):
    lead = rows.shape[:-1]
    return jnp.swapaxes(rows.reshape(lead + (4, 4, 2, 48)), -3, -2).reshape(rows.shape)


def join_positions(tensor, own):
    other = swap(own, "tensor")
    return jnp.concatenate(
        [pick(tensor, own, other), pick(tensor, other, own)], axis=1
    ).reshape(384, WIDTH)


def own_positions(tensor, rows):
    rows = rows.reshape(3, 128, 1536)
    return pick(tensor, rows[:, :64], rows[:, 64:])


def per_device(
    inputs, cotangent, plan, attn_gain, mlp_gain, w_query, key_weight, value_weight,
    w_out, w_gate, w_up, w_down,
):
    core = lax.axis_index("section")
    z_low = lax.axis_index("zl")
    tensor = lax.axis_index("tensor")

    attn_scale = attn_gain[0].astype(F32)[:, None]
    mlp_scale = mlp_gain[0].astype(F32)[:, None]

    core_ref = core.astype(jnp.int32).reshape(1)
    mine, give = pack_shards(
        core_ref, attn_gain, mlp_gain,
        w_gate[0], w_up[0], w_down[0].T, w_query[0], key_weight[0], value_weight[0], w_out[0].T,
    )
    got = swap(give, "section")
    layer_zero, layer_one = pick(core, mine, got), pick(core, got, mine)
    first_weights = gather_rows(
        z_low, jnp.concatenate([layer_zero, layer_one[:, MLP_COLS:]], axis=1)
    )
    last_weights = gather_rows(z_low, layer_one[:, :MLP_COLS])

    stream = join_positions(tensor, to_ring_order(inputs[:, 0][plan]))
    stream, late = lax.optimization_barrier((stream, cotangent))
    out_grad = join_positions(tensor, to_ring_order(late[:, 0][plan]))
    stream, out_grad = lax.optimization_barrier((stream, out_grad))

    def whole_rows(sums):
        own, other = jnp.concatenate(sums[:PARTS]), jnp.concatenate(sums[PARTS:])
        return jnp.concatenate([pick(core, own, other), pick(core, other, own)], axis=1).astype(F32)

    x_zero = stream
    first_zero, qkv_zero, prob_zero, mix_zero, *partial = attention_first(
        core_ref, x_zero, first_weights, MLP_COLS
    )
    near, token = fetch(first_weights, 0, MLP_COLS)
    sums, token = sum_four(partial, beside=token)
    middle_zero, second_zero, gate_zero, up_zero, hidden_zero, *partial = mlp_forward(
        core_ref, x_zero, sums, near, token
    )
    near, token = fetch(first_weights, LAYER_COLS, ATTN_COLS)
    sums, token = sum_four(partial, beside=token)
    x_one, first_one, qkv_one, prob_one, mix_one, *partial = attention_next(
        core_ref, middle_zero, sums, near, token
    )
    sums, ahead = sum_four(partial, within=lambda tie: mlp_ahead(out_grad, tie(last_weights)))
    hidden_grad, near, token = ahead

    middle_one, hidden_far, second_one, hidden_one, pair_grad = mlp_last(
        core_ref, x_one, sums, hidden_grad, near, token
    )
    one_mlp, done = mlp_weights(None, MLP_COLS, second_one, out_grad, pair_grad, hidden_one)
    last_pair = scatter_pair(one_mlp)
    partial = mlp_in(core_ref, pair_grad, last_weights, done)
    near, token = fetch(first_weights, LAYER_COLS, ATTN_COLS, one_mlp)
    sums, token = sum_four(partial, beside=token)
    middle_grad, attn_in, qkv_grad, *partial = attention_backward(
        core_ref, out_grad, middle_one, sums, qkv_one, prob_one, near, token, True
    )
    buffer, _ = attention_weights(None, REST_COLS, MLP_COLS, first_one, attn_in, qkv_grad, mix_one)
    near, token = fetch(first_weights, 0, MLP_COLS, buffer)
    sums, (buffer, token) = sum_four(partial, beside=(buffer, token))

    grad_one, pair_grad, *partial = mlp_backward(
        core_ref, (x_one, middle_grad, *sums), gate_zero, up_zero, near, token
    )
    buffer, _ = mlp_weights(buffer, REST_COLS, second_zero, grad_one, pair_grad, hidden_zero)
    near, token = fetch(first_weights, MLP_COLS, ATTN_COLS, buffer)
    sums, (buffer, token) = sum_four(partial, beside=(buffer, token))
    hidden_far, sums[0] = lax.optimization_barrier((hidden_far, sums[0]))
    down_partial = mlp_down(core_ref, hidden_far, last_weights)
    middle_grad, attn_in, qkv_grad = attention_backward(
        core_ref, grad_one, middle_zero, sums, qkv_zero, prob_zero, near, token, False
    )
    buffer, done = attention_weights(
        buffer, REST_COLS, LAYER_COLS, first_zero, attn_in, qkv_grad, mix_zero
    )
    rest_pair = scatter_pair(buffer)
    sums, _ = sum_four(attention_in(core_ref, qkv_grad, near, done))
    rows = x_zero.astype(F32)
    grad_zero = middle_grad + norm_back(whole_rows(sums), rows, inverse_norm(rows))
    down_sums, _ = sum_four(down_partial)
    result_one = (middle_one + whole_rows(down_sums)).astype(BF16)
    outputs = [own_positions(tensor, x_one), own_positions(tensor, result_one)]
    grads = [own_positions(tensor, grad_zero.astype(BF16)), own_positions(tensor, grad_one)]

    layer_outputs = from_ring_order(pick(core, outputs[0], outputs[1]))
    input_grads = from_ring_order(pick(core, grads[0], grads[1]))
    last_grad = scatter_low(z_low, last_pair)
    rest_pair, layer_outputs, input_grads, last_grad = lax.optimization_barrier(
        (rest_pair, layer_outputs, input_grads, last_grad)
    )
    keep = pick(z_low, rest_pair[:48], rest_pair[48:])
    arrived = swap(pick(z_low, rest_pair[48:], rest_pair[:48]), "zl")
    mine, give, terms = combine_grads(
        core_ref, keep, arrived, last_grad, layer_zero, layer_one
    )
    got = swap(give, "section")
    arrived = swap(terms, "tensor")
    gate_grad, up_grad, down_grad, query_grad, key_grad, value_grad, out_weight_grad = unpack_grads(
        core_ref, attn_scale, mlp_scale, mine, got
    )
    arrived, key_grad = lax.optimization_barrier((arrived, key_grad))
    terms = terms + arrived
    terms = pick(core, terms[:2], terms[2:]) + swap(pick(core, terms[2:], terms[:2]), "section")
    return (
        layer_outputs[None, :, None],
        input_grads[None, :, None],
        (terms[0] / attn_scale[:, 0])[None],
        (terms[1] / mlp_scale[:, 0])[None],
        query_grad[None],
        key_grad[None],
        value_grad[None],
        out_weight_grad.T[None],
        gate_grad[None],
        up_grad[None],
        down_grad.T[None],
    )


def solution(mesh):
    split = Mesh(mesh.devices.reshape(2, 4, 2, 4, 2), ("section", "y", "zl", "x", "tensor"))
    dp = ("y", "zl", "x")
    rows = P("section", dp, "tensor")
    columns = P("section", "tensor", dp)
    return jax.shard_map(
        per_device,
        mesh=split,
        in_specs=(
            P(None, dp, "tensor", None),
            P(None, dp, "tensor", None),
            P(),
            P("section", dp),
            P("section", dp),
            rows,
            rows,
            rows,
            columns,
            rows,
            rows,
            columns,
        ),
        out_specs=(
            P("section", None, dp, "tensor", None),
            P("section", None, dp, "tensor", None),
            P("section", dp),
            P("section", dp),
            rows,
            rows,
            rows,
            columns,
            rows,
            rows,
            columns,
        ),
        check_vma=False,
    )
```

profile of v0, /device:TPU:1, one launch (start us, length us, event | category | flops | bytes accessed | tf_op | source)
XLA Modules:
  0.0 463.2 jit_solution(7078499977779622927)
XLA Ops:
  7.2 2.2 pack_shards.1
  14.3 11.8 %collective-permute-done.3 = bf16[48,5376]{1,0:T(8,128)(2,1)S(1)} collective-permute-done((bf16[48,5376]{1,0:T(8,128)(2,1)S(1)}, bf16[48,5376]{1,0:T(8,128)(2,1)S(1)}, u32[]{:S(2)}, u32[]{:S(2)}) %collective-permute-start.3) | collective-permute-done | bytes 516128 | tf_op jit(solution)/shard_map/ppermute | solution.py:34
  28.7 6.4 %collective-permute-done.18 = bf16[48,3072]{1,0:T(8,128)(2,1)S(1)} collective-permute-done((bf16[48,3072]{1,0:T(8,128)(2,1)S(1)}, bf16[48,3072]{1,0:T(8,128)(2,1)S(1)}, u32[]{:S(2)}, u32[]{:S(2)}) %collective-permute-start.18) | collective-permute-done | bytes 294944 | tf_op jit(solution)/shard_map/ppermute | solution.py:34
  38.4 2.8 copy.31
  41.2 3.9 reshape.105
  45.0 2.9 collective-permute-start
  48.0 11.7 %collective-permute-done = bf16[3,64,1536]{2,1,0:T(8,128)(2,1)S(1)} collective-permute-done((bf16[3,64,1536]{2,1,0:T(8,128)(2,1)S(1)}, bf16[3,64,1536]{2,1,0:T(8,128)(2,1)S(1)}, u32[]{:S(2)}, u32[]{:S(2)}) %collective-permute-start) | collective-permute-done | bytes 589856 | tf_op jit(solution)/shard_map/ppermute | solution.py:34
  61.5 2.5 reshape.107
  64.0 4.2 copy.32
  68.2 3.9 reshape.108
  72.0 3.2 collective-permute-start.1
  75.2 10.7 %collective-permute-done.1 = bf16[3,64,1536]{2,1,0:T(8,128)(2,1)S(1)} collective-permute-done((bf16[3,64,1536]{2,1,0:T(8,128)(2,1)S(1)}, bf16[3,64,1536]{2,1,0:T(8,128)(2,1)S(1)}, u32[]{:S(2)}, u32[]{:S(2)}) %collective-permute-start.1) | collective-permute-done | bytes 589856 | tf_op jit(solution)/shard_map/ppermute | solution.py:34
  86.1 53.6 %all-gather.3.cloned.1.call-done.w_any = bf16[1536,5376]{1,0:T(8,128)(2,1)} async-done(((bf16[96,5376]{1,0:T(8,128)(2,1)}), bf16[1536,5376]{1,0:T(8,128)(2,1)}) %all-gather.3.cloned.1.call-update) | async-done | bytes 16515088 | tf_op jit(solution)/shard_map/all_gather | solution.py:864
  139.8 6.9 %attention_first.1 = (bf16[384,1536]{1,0:T(8,128)(2,1)}, bf16[384,768]{1,0:T(8,128)(2,1)}, f32[6,256,128]{2,1,0:T(8,128)}, bf16[384,384]{1,0:T(8,128)(2,1)S(1)},...) custom-call(s32[1]{0:T(128)} %bitcast.core_ref, ...), custom_call_target="tpu_custom_call" | custom-call | flops 1358954496 | bytes 8000000 | tf_op jit(solution)/shard_map/attention_first/pallas_call | solution.py:261
  148.7 3.0 collective-permute-start.5
  152.1 3.9 fetch.5
  156.0 2.5 collective-permute-done.5
  158.6 2.1 collective-permute-start.8
  160.7 4.2 collective-permute-done.7
  167.4 5.2 %mlp_forward.1 = (f32[384,1536]{1,0:T(8,128)}, bf16[384,1536]{1,0:T(8,128)(2,1)}, f32[384,1024]{1,0:T(8,128)}, f32[384,1024]{1,0:T(8,128)}, bf16[384,1024]{1,0:T...) custom-call(s32[1]{0:T(128)} %bitcast.core_ref, ...), custom_call_target="tpu_custom_call" | custom-call | flops 3623878656 | bytes 15000000 | tf_op jit(solution)/shard_map/mlp_forward/pallas_call | solution.py:367
  174.4 3.0 collective-permute-start.11
  177.8 2.2 fetch.6
  179.9 4.2 collective-permute-done.11
  184.3 2.1 collective-permute-start.14
  186.3 4.2 collective-permute-done.13
  193.1 4.9 %attention_next.1 = (bf16[384,1536]{1,0:T(8,128)(2,1)}, bf16[384,1536]{1,0:T(8,128)(2,1)}, bf16[384,768]{1,0:T(8,128)(2,1)}, f32[6,256,128]{2,1,0:T(8,128)}, bf1...) custom-call(s32[1]{0:T(128)} %bitcast.core_ref, ...), custom_call_target="tpu_custom_call" | custom-call | flops 1358954496 | bytes 8000000 | tf_op jit(solution)/shard_map/attention_next/pallas_call | solution.py:283
  199.7 3.0 collective-permute-start.17
  203.7 5.8 %collective-permute-done.17 = bf16[192,768]{1,0:T(8,128)(2,1)S(1)} collective-permute-done((bf16[192,768]{1,0:T(8,128)(2,1)S(1)}, bf16[192,768]{1,0:T(8,128)(2,1)S(1)}, u32[]{:S(2)}, u32[]{:S(2)}) %collective-permute-start.17) | collective-permute-done | bytes 294944 | tf_op jit(solution)/shard_map/ppermute | solution.py:34
  209.6 7.7 %all-gather.5.cloned.1.call-done.w_any = bf16[1536,3072]{1,0:T(8,128)(2,1)} async-done(((bf16[96,3072]{1,0:T(8,128)(2,1)}), bf16[1536,3072]{1,0:T(8,128)(2,1)}) %all-gather.5.cloned.1.call-update) | async-done | bytes 9437200 | tf_op jit(solution)/shard_map/all_gather | solution.py:864
  219.3 3.8 mlp_ahead.1
  223.2 4.5 mlp_last.1
  227.8 7.1 %mlp_weights.2 = (bf16[1536,3072]{1,0:T(8,128)(2,1)}, f32[8,128]{1,0:T(8,128)S(1)}) custom-call(bf16[384,1536]{1,0:T(8,128)(2,1)S(1)} %get-tuple-element.163.second_ref, bf16[384,1536]{1,0:T(8,128)(2,1)S(1)} %bitcast.52, bf16[384,2048]{1,0:T(8,128)(2,1)S(1)} %get-tuple-element.162.pair_grad_ref, bf16[384,1024]{1,0:T(8,128)(2,1)S(1)} %get-tuple-element.164.hidden_ref), custom_call_target="tpu_custom_call" | custom-call | flops 3623878656 | bytes 14495514 | tf_op jit(solution)/shard_map/mlp_weights/pallas_call | solution.py:681
  236.3 5.6 %mlp_in.1 = (bf16[192,768]{1,0:T(8,128)(2,1)S(1)}, bf16[192,768]{1,0:T(8,128)(2,1)S(1)}, bf16[192,768]{1,0:T(8,128)(2,1)S(1)}, bf16[192,768]{1,0:T(8,128)(2,1)S(1)}) custom-call(s32[1]{0:T(128)} %bitcast.core_ref, bf16[384,2048]{1,0:T(8,128)(2,1)S(1)} %copy-done.16, bf16[1536,3072]{1,0:T(8,128)(2,1)} %all-gather.5.cloned.1.call-done.w_any, ...), custom_call_target="tpu_custom_call" | custom-call | flops 2415919104 | bytes 9000000 | tf_op jit(solution)/shard_map/mlp_in/pallas_call | solution.py:510
  243.8 2.9 collective-permute-start.24
  247.1 2.2 fetch.7
  249.3 4.2 collective-permute-done.24
  253.6 2.1 collective-permute-start.27
  255.7 4.2 collective-permute-done.26
  262.7 5.9 %attention_backward.2 = (f32[384,1536]{1,0:T(8,128)S(1)}, bf16[384,1536]{1,0:T(8,128)(2,1)S(1)}, bf16[384,768]{1,0:T(8,128)(2,1)S(1)}, bf16[192,768]{1,0:T(8,128...) custom-call(s32[1]{0:T(128)} %bitcast.core_ref, ...), custom_call_target="tpu_custom_call" | custom-call | flops 1358954496 | bytes 8000000 | tf_op jit(solution)/shard_map/attention_backward/pallas_call | solution.py:627
  270.3 2.9 collective-permute-start.30
  273.7 4.0 attention_weights.2
  277.7 4.4 fetch.8
  282.6 3.8 collective-permute-done.32
  289.0 5.4 %mlp_backward.1 = (bf16[384,1536]{1,0:T(8,128)(2,1)S(1)}, bf16[384,2048]{1,0:T(8,128)(2,1)S(1)}, bf16[192,768]{1,0:T(8,128)(2,1)S(1)}, bf16[192,768]{1,0:T(8,128...) custom-call(s32[1]{0:T(128)} %bitcast.core_ref, bf16[384,1536]{1,0:T(8,128)(2,1)S(1)} %copy-done.9, ...), custom_call_target="tpu_custom_call" | custom-call | flops 3623878656 | bytes 15000000 | tf_op jit(solution)/shard_map/mlp_backward/pallas_call | solution.py:408
  296.5 2.9 collective-permute-start.36
  299.9 7.8 %mlp_weights.3 = (bf16[1536,5376]{1,0:T(8,128)(2,1)}, f32[8,128]{1,0:T(8,128)}) custom-call(bf16[384,1536]{1,0:T(8,128)(2,1)S(1)} %copy-done.18, bf16[384,1536]{1,0:T(8,128)(2,1)S(1)} %get-tuple-element.193.g_ref, bf16[384,2048]{1,0:T(8,128)(2,1)S(1)} %get-tuple-element.201.pair_grad_ref, ...), custom_call_target="tpu_custom_call", output_to_operand_aliasing={{0}: (4, {})} | custom-call | flops 3623878656 | bytes 14495514 | tf_op jit(solution)/shard_map/mlp_weights/pallas_call | solution.py:681
  307.7 2.2 fetch.9
  315.2 6.3 %attention_backward.3 = (f32[384,1536]{1,0:T(8,128)}, bf16[384,1536]{1,0:T(8,128)(2,1)S(1)}, bf16[384,768]{1,0:T(8,128)(2,1)S(1)}) custom-call(s32[1]{0:T(128)} %bitcast.core_ref, bf16[384,1536]{1,0:T(8,128)(2,1)S(1)} %get-tuple-element.193.g_ref, f32[384,1536]{1,0:T(8,128)S(1)} %copy-done.5, bf16[192,768]{1,0:T(8,128)(2,1)S(1)} %add_convert_fusion.12.rest_0_, ...), custom_call_target="tpu_custom_call" | custom-call | flops 1358954496 | bytes 8000000 | tf_op jit(solution)/shard_map/attention_backward/pallas_call | solution.py:627
  321.6 3.4 attention_weights.3
  326.2 3.5 mlp_down.1
  331.6 3.0 collective-permute-start.42
  337.0 4.4 collective-permute-done.42
  343.7 3.0 collective-permute-start.48
  349.6 4.7 %collective-permute-done.48 = bf16[192,768]{1,0:T(8,128)(2,1)S(1)} collective-permute-done((bf16[192,768]{1,0:T(8,128)(2,1)S(1)}, bf16[192,768]{1,0:T(8,128)(2,1)S(1)}, u32[]{:S(2)}, u32[]{:S(2)}) %collective-permute-start.48) | collective-permute-done | bytes 294944 | tf_op jit(solution)/shard_map/ppermute | solution.py:34
  355.9 4.7 %collective-permute-done.50 = bf16[192,768]{1,0:T(8,128)(2,1)S(1)} collective-permute-done((bf16[192,768]{1,0:T(8,128)(2,1)S(1)}, bf16[192,768]{1,0:T(8,128)(2,1)S(1)}, u32[]{:S(2)}, u32[]{:S(2)}) %collective-permute-start.50) | collective-permute-done | bytes 294944 | tf_op jit(solution)/shard_map/ppermute | solution.py:34
  366.3 3.4 reshape.112
  369.7 3.3 copy.33
  373.0 4.6 reshape.113
  387.0 2.2 fusion.6
  389.2 2.5 reshape.116
  393.4 4.6 reshape.117
  399.1 34.6 %reduce-scatter.3.cloned.1.call-done = bf16[96,5376]{1,0:T(8,128)(2,1)} async-done(((bf16[1536,5376]{1,0:T(8,128)(2,1)}), bf16[96,5376]{1,0:T(8,128)(2,1)}) %reduce-scatter.3.cloned.1.call-update) | async-done | bytes 1032208 | tf_op jit(solution)/shard_map/reduce_scatter | solution.py:868
  436.5 10.9 %collective-permute-done.54.arrived_ref = bf16[48,5376]{1,0:T(8,128)(2,1)S(1)} collective-permute-done((bf16[48,5376]{1,0:T(8,128)(2,1)S(1)}, bf16[48,5376]{1,0:T(8,128)(2,1)S(1)}, u32[]{:S(2)}, u32[]{:S(2)}) %collective-permute-start.54) | collective-permute-done | bytes 516128 | tf_op jit(solution)/shard_map/ppermute | solution.py:34
  449.8 2.9 collective-permute-start.55
  (234 shorter events, 86.1 us)
Async XLA Ops:
  7.2 29.0 %copy-start = (bf16[3,1,64,1536]{3,2,1,0:T(8,128)(2,1)S(1)}, bf16[3,1,64,1536]{3,2,1,0:T(8,128)(2,1)}, u32[]{:S(2)}) copy-start(bf16[3,1,64,1536]{3,2,1,0:T(8,128)(2,1)} %param.12) | copy-start | bytes 1769476
  7.2 132.6 %all-gather.3.cloned.1.call-start = ((), (), s32[]{:S(2)}) async-start(), calls=%async_computation.2 | async-start | bytes 17547264 | tf_op jit(solution)/shard_map/all_gather | solution.py:864
  9.5 2.9 collective-permute-start.2
  12.5 13.6 %collective-permute-start.3 = (bf16[48,5376]{1,0:T(8,128)(2,1)S(1)}, bf16[48,5376]{1,0:T(8,128)(2,1)S(1)}, u32[]{:S(2)}, u32[]{:S(2)}) collective-permute-start(bf16[48,5376]{1,0:T(8,128)(2,1)S(1)} %pad_maximum_fusion.7), channel_id=1, source_target_pairs={{0,8},{8,0},{1,9},{9,1},{2,10},{10,2},{3,11},{11,3},{4,12},{12,4},... | collective-permute-start | bytes 1548296 | tf_op jit(solution)/shard_map/ppermute | solution.py:34
  27.4 189.9 %all-gather.5.cloned.1.call-start = ((), (), s32[]{:S(2)}) async-start(), calls=%async_computation.3 | async-start | bytes 10027008 | tf_op jit(solution)/shard_map/all_gather | solution.py:864
  27.4 7.7 %collective-permute-start.18 = (bf16[48,3072]{1,0:T(8,128)(2,1)S(1)}, bf16[48,3072]{1,0:T(8,128)(2,1)S(1)}, u32[]{:S(2)}, u32[]{:S(2)}) collective-permute-start(bf16[48,3072]{1,0:T(8,128)(2,1)S(1)} %slice.83), channel_id=1, source_target_pairs={{0,8},{8,0},{1,9},{9,1},{2,10},{10,2},{3,11},{11,3},{4,12},{12,4},... | collective-permute-start | bytes 884744 | tf_op jit(solution)/shard_map/ppermute | solution.py:34
  36.1 348.1 %reduce-scatter.5.cloned.1.call-start = ((), (), s32[]{:S(2)}) async-start(), calls=%async_computation.5 | async-start | bytes 10027008 | tf_op jit(solution)/shard_map/reduce_scatter | solution.py:868
  45.0 14.6 %collective-permute-start = (bf16[3,64,1536]{2,1,0:T(8,128)(2,1)S(1)}, bf16[3,64,1536]{2,1,0:T(8,128)(2,1)S(1)}, u32[]{:S(2)}, u32[]{:S(2)}) collective-permute-start(bf16[3,64,1536]{2,1,0:T(8,128)(2,1)S(1)} %reshape.105), channel_id=1, source_target_pairs={{0,1},{1,0},{2,3},{3,2},{4,5},{5,4},{6,7},{7,6},{8,9},{9,8},{10,11... | collective-permute-start | bytes 1769480 | tf_op jit(solution)/shard_map/ppermute | solution.py:34
  72.0 13.9 %collective-permute-start.1 = (bf16[3,64,1536]{2,1,0:T(8,128)(2,1)S(1)}, bf16[3,64,1536]{2,1,0:T(8,128)(2,1)S(1)}, u32[]{:S(2)}, u32[]{:S(2)}) collective-permute-start(bf16[3,64,1536]{2,1,0:T(8,128)(2,1)S(1)} %reshape.108), channel_id=1, source_target_pairs={{0,1},{1,0},{2,3},{3,2},{4,5},{5,4},{6,7},{7,6},{8,9},{9,8},{10,11... | collective-permute-start | bytes 1769480 | tf_op jit(solution)/shard_map/ppermute | solution.py:34
  146.7 2.0 collective-permute-start.4
  147.5 4.2 collective-permute-start.6
  148.7 9.8 %collective-permute-start.5 = (bf16[192,768]{1,0:T(8,128)(2,1)S(1)}, bf16[192,768]{1,0:T(8,128)(2,1)S(1)}, u32[]{:S(2)}, u32[]{:S(2)}) collective-permute-start(bf16[192,768]{1,0:T(8,128)(2,1)S(1)} %add_convert_fusion.33), channel_id=1, source_target_pairs={{0,1},{1,0},{2,3},{3,2},{4,5},{5,4},{6,7},{7,6},{8,9},{9,8},{10,11... | collective-permute-start | bytes 884744 | tf_op jit(solution)/shard_map/ppermute | solution.py:34
  151.8 13.1 %collective-permute-start.7 = (bf16[192,768]{1,0:T(8,128)(2,1)S(1)}, bf16[192,768]{1,0:T(8,128)(2,1)S(1)}, u32[]{:S(2)}, u32[]{:S(2)}) collective-permute-start(bf16[192,768]{1,0:T(8,128)(2,1)S(1)} %add_convert_fusion.31), channel_id=1, source_target_pairs={{0,1},{1,0},{2,3},{3,2},{4,5},{5,4},{6,7},{7,6},{8,9},{9,8},{10,11... | collective-permute-start | bytes 884744 | tf_op jit(solution)/shard_map/ppermute | solution.py:34
  158.6 7.6 %collective-permute-start.8 = (bf16[192,768]{1,0:T(8,128)(2,1)S(1)}, bf16[192,768]{1,0:T(8,128)(2,1)S(1)}, u32[]{:S(2)}, u32[]{:S(2)}) collective-permute-start(bf16[192,768]{1,0:T(8,128)(2,1)S(1)} %add_convert_fusion.32.rest_0_), channel_id=1, source_target_pairs={{0,64},{64,0},{1,65},{65,1},{2,66},{66,2},{3,67},{67,3},{4,68},{68... | collective-permute-start | bytes 884744 | tf_op jit(solution)/shard_map/ppermute | solution.py:34
  164.9 2.5 collective-permute-start.9
  172.6 1.7 collective-permute-start.10
  173.1 4.2 collective-permute-start.12
  174.4 9.8 %collective-permute-start.11 = (bf16[192,768]{1,0:T(8,128)(2,1)S(1)}, bf16[192,768]{1,0:T(8,128)(2,1)S(1)}, u32[]{:S(2)}, u32[]{:S(2)}) collective-permute-start(bf16[192,768]{1,0:T(8,128)(2,1)S(1)} %add_convert_fusion.29), channel_id=1, source_target_pairs={{0,1},{1,0},{2,3},{3,2},{4,5},{5,4},{6,7},{7,6},{8,9},{9,8},{10,11... | collective-permute-start | bytes 884744 | tf_op jit(solution)/shard_map/ppermute | solution.py:34
  177.4 13.1 %collective-permute-start.13 = (bf16[192,768]{1,0:T(8,128)(2,1)S(1)}, bf16[192,768]{1,0:T(8,128)(2,1)S(1)}, u32[]{:S(2)}, u32[]{:S(2)}) collective-permute-start(bf16[192,768]{1,0:T(8,128)(2,1)S(1)} %add_convert_fusion.27), channel_id=1, source_target_pairs={{0,1},{1,0},{2,3},{3,2},{4,5},{5,4},{6,7},{7,6},{8,9},{9,8},{10,11... | collective-permute-start | bytes 884744 | tf_op jit(solution)/shard_map/ppermute | solution.py:34
  184.3 7.6 %collective-permute-start.14 = (bf16[192,768]{1,0:T(8,128)(2,1)S(1)}, bf16[192,768]{1,0:T(8,128)(2,1)S(1)}, u32[]{:S(2)}, u32[]{:S(2)}) collective-permute-start(bf16[192,768]{1,0:T(8,128)(2,1)S(1)} %add_convert_fusion.28.rest_0_), channel_id=1, source_target_pairs={{0,64},{64,0},{1,65},{65,1},{2,66},{66,2},{3,67},{67,3},{4,68},{68... | collective-permute-start | bytes 884744 | tf_op jit(solution)/shard_map/ppermute | solution.py:34
  190.6 2.5 collective-permute-start.15
  198.0 1.7 collective-permute-start.16
  198.4 4.3 collective-permute-start.19
  199.7 9.8 %collective-permute-start.17 = (bf16[192,768]{1,0:T(8,128)(2,1)S(1)}, bf16[192,768]{1,0:T(8,128)(2,1)S(1)}, u32[]{:S(2)}, u32[]{:S(2)}) collective-permute-start(bf16[192,768]{1,0:T(8,128)(2,1)S(1)} %add_convert_fusion.25), channel_id=1, source_target_pairs={{0,1},{1,0},{2,3},{3,2},{4,5},{5,4},{6,7},{7,6},{8,9},{9,8},{10,11... | collective-permute-start | bytes 884744 | tf_op jit(solution)/shard_map/ppermute | solution.py:34
  203.5 14.5 %collective-permute-start.20 = (bf16[192,768]{1,0:T(8,128)(2,1)}, bf16[192,768]{1,0:T(8,128)(2,1)}, u32[]{:S(2)}, u32[]{:S(2)}) collective-permute-start(bf16[192,768]{1,0:T(8,128)(2,1)} %add_convert_fusion.23), channel_id=1, source_target_pairs={{0,1},{1,0},{2,3},{3,2},{4,5},{5,4},{6,7},{7,6},{8,9},{9,8},{10,11... | collective-permute-start | bytes 884744 | tf_op jit(solution)/shard_map/ppermute | solution.py:34
  217.3 5.9 %collective-permute-start.21 = (bf16[192,768]{1,0:T(8,128)(2,1)S(1)}, bf16[192,768]{1,0:T(8,128)(2,1)S(1)}, u32[]{:S(2)}, u32[]{:S(2)}) collective-permute-start(bf16[192,768]{1,0:T(8,128)(2,1)S(1)} %add_convert_fusion.24.rest_0_), channel_id=1, source_target_pairs={{0,64},{64,0},{1,65},{65,1},{2,66},{66,2},{3,67},{67,3},{4,68},{68... | collective-permute-start | bytes 884744 | tf_op jit(solution)/shard_map/ppermute | solution.py:34
  219.1 4.1 collective-permute-start.22
  234.9 198.8 %reduce-scatter.3.cloned.1.call-start = ((), (), s32[]{:S(2)}) async-start(), calls=%async_computation.4 | async-start | bytes 17547264 | tf_op jit(solution)/shard_map/reduce_scatter | solution.py:868
  242.0 1.7 collective-permute-start.23
  242.5 4.2 collective-permute-start.25
  243.8 9.8 %collective-permute-start.24 = (bf16[192,768]{1,0:T(8,128)(2,1)S(1)}, bf16[192,768]{1,0:T(8,128)(2,1)S(1)}, u32[]{:S(2)}, u32[]{:S(2)}) collective-permute-start(bf16[192,768]{1,0:T(8,128)(2,1)S(1)} %add_convert_fusion.21), channel_id=1, source_target_pairs={{0,1},{1,0},{2,3},{3,2},{4,5},{5,4},{6,7},{7,6},{8,9},{9,8},{10,11... | collective-permute-start | bytes 884744 | tf_op jit(solution)/shard_map/ppermute | solution.py:34
  246.8 13.1 %collective-permute-start.26 = (bf16[192,768]{1,0:T(8,128)(2,1)S(1)}, bf16[192,768]{1,0:T(8,128)(2,1)S(1)}, u32[]{:S(2)}, u32[]{:S(2)}) collective-permute-start(bf16[192,768]{1,0:T(8,128)(2,1)S(1)} %add_convert_fusion.19), channel_id=1, source_target_pairs={{0,1},{1,0},{2,3},{3,2},{4,5},{5,4},{6,7},{7,6},{8,9},{9,8},{10,11... | collective-permute-start | bytes 884744 | tf_op jit(solution)/shard_map/ppermute | solution.py:34
  253.6 7.8 %collective-permute-start.27 = (bf16[192,768]{1,0:T(8,128)(2,1)S(1)}, bf16[192,768]{1,0:T(8,128)(2,1)S(1)}, u32[]{:S(2)}, u32[]{:S(2)}) collective-permute-start(bf16[192,768]{1,0:T(8,128)(2,1)S(1)} %add_convert_fusion.20.rest_0_), channel_id=1, source_target_pairs={{0,64},{64,0},{1,65},{65,1},{2,66},{66,2},{3,67},{67,3},{4,68},{68... | collective-permute-start | bytes 884744 | tf_op jit(solution)/shard_map/ppermute | solution.py:34
  260.0 2.7 collective-permute-start.28
  268.6 1.7 collective-permute-start.29
  269.0 4.2 collective-permute-start.31
  270.3 11.8 %collective-permute-start.30 = (bf16[192,768]{1,0:T(8,128)(2,1)S(1)}, bf16[192,768]{1,0:T(8,128)(2,1)S(1)}, u32[]{:S(2)}, u32[]{:S(2)}) collective-permute-start(bf16[192,768]{1,0:T(8,128)(2,1)S(1)} %add_convert_fusion.17), channel_id=1, source_target_pairs={{0,1},{1,0},{2,3},{3,2},{4,5},{5,4},{6,7},{7,6},{8,9},{9,8},{10,11... | collective-permute-start | bytes 884744 | tf_op jit(solution)/shard_map/ppermute | solution.py:34
  273.3 13.1 %collective-permute-start.32 = (bf16[192,768]{1,0:T(8,128)(2,1)S(1)}, bf16[192,768]{1,0:T(8,128)(2,1)S(1)}, u32[]{:S(2)}, u32[]{:S(2)}) collective-permute-start(bf16[192,768]{1,0:T(8,128)(2,1)S(1)} %add_convert_fusion.15), channel_id=1, source_target_pairs={{0,1},{1,0},{2,3},{3,2},{4,5},{5,4},{6,7},{7,6},{8,9},{9,8},{10,11... | collective-permute-start | bytes 884744 | tf_op jit(solution)/shard_map/ppermute | solution.py:34
  282.2 5.6 %collective-permute-start.33 = (bf16[192,768]{1,0:T(8,128)(2,1)S(1)}, bf16[192,768]{1,0:T(8,128)(2,1)S(1)}, u32[]{:S(2)}, u32[]{:S(2)}) collective-permute-start(bf16[192,768]{1,0:T(8,128)(2,1)S(1)} %add_convert_fusion.16.rest_0_), channel_id=1, source_target_pairs={{0,64},{64,0},{1,65},{65,1},{2,66},{66,2},{3,67},{67,3},{4,68},{68... | collective-permute-start | bytes 884744 | tf_op jit(solution)/shard_map/ppermute | solution.py:34
  286.5 2.5 collective-permute-start.34
  294.4 2.1 collective-permute-start.35
  295.2 4.2 collective-permute-start.37
  296.5 13.3 %collective-permute-start.36 = (bf16[192,768]{1,0:T(8,128)(2,1)S(1)}, bf16[192,768]{1,0:T(8,128)(2,1)S(1)}, u32[]{:S(2)}, u32[]{:S(2)}) collective-permute-start(bf16[192,768]{1,0:T(8,128)(2,1)S(1)} %add_convert_fusion.13), channel_id=1, source_target_pairs={{0,1},{1,0},{2,3},{3,2},{4,5},{5,4},{6,7},{7,6},{8,9},{9,8},{10,11... | collective-permute-start | bytes 884744 | tf_op jit(solution)/shard_map/ppermute | solution.py:34
  299.6 13.1 %collective-permute-start.38 = (bf16[192,768]{1,0:T(8,128)(2,1)S(1)}, bf16[192,768]{1,0:T(8,128)(2,1)S(1)}, u32[]{:S(2)}, u32[]{:S(2)}) collective-permute-start(bf16[192,768]{1,0:T(8,128)(2,1)S(1)} %add_convert_fusion.11), channel_id=1, source_target_pairs={{0,1},{1,0},{2,3},{3,2},{4,5},{5,4},{6,7},{7,6},{8,9},{9,8},{10,11... | collective-permute-start | bytes 884744 | tf_op jit(solution)/shard_map/ppermute | solution.py:34
  310.0 4.1 collective-permute-start.39
  312.7 2.5 collective-permute-start.40
  329.7 1.8 collective-permute-start.41
  330.6 5.8 %collective-permute-start.43 = (bf16[192,768]{1,0:T(8,128)(2,1)S(1)}, bf16[192,768]{1,0:T(8,128)(2,1)S(1)}, u32[]{:S(2)}, u32[]{:S(2)}) collective-permute-start(bf16[192,768]{1,0:T(8,128)(2,1)S(1)} %get-tuple-element.220), channel_id=1, source_target_pairs={{0,64},{64,0},{1,65},{65,1},{2,66},{66,2},{3,67},{67,3},{4,68},{68... | collective-permute-start | bytes 884744 | tf_op jit(solution)/shard_map/ppermute | solution.py:34
  331.6 9.8 %collective-permute-start.42 = (bf16[192,768]{1,0:T(8,128)(2,1)S(1)}, bf16[192,768]{1,0:T(8,128)(2,1)S(1)}, u32[]{:S(2)}, u32[]{:S(2)}) collective-permute-start(bf16[192,768]{1,0:T(8,128)(2,1)S(1)} %add_convert_fusion.9), channel_id=1, source_target_pairs={{0,1},{1,0},{2,3},{3,2},{4,5},{5,4},{6,7},{7,6},{8,9},{9,8},{10,11... | collective-permute-start | bytes 884744 | tf_op jit(solution)/shard_map/ppermute | solution.py:34
  335.7 7.9 %collective-permute-start.47 = (bf16[192,768]{1,0:T(8,128)(2,1)S(1)}, bf16[192,768]{1,0:T(8,128)(2,1)S(1)}, u32[]{:S(2)}, u32[]{:S(2)}) collective-permute-start(bf16[192,768]{1,0:T(8,128)(2,1)S(1)} %get-tuple-element.224), channel_id=1, source_target_pairs={{0,64},{64,0},{1,65},{65,1},{2,66},{66,2},{3,67},{67,3},{4,68},{68... | collective-permute-start | bytes 884744 | tf_op jit(solution)/shard_map/ppermute | solution.py:34
  336.5 11.2 %collective-permute-start.44 = (bf16[192,768]{1,0:T(8,128)(2,1)S(1)}, bf16[192,768]{1,0:T(8,128)(2,1)S(1)}, u32[]{:S(2)}, u32[]{:S(2)}) collective-permute-start(bf16[192,768]{1,0:T(8,128)(2,1)S(1)} %add_convert_fusion.7), channel_id=1, source_target_pairs={{0,1},{1,0},{2,3},{3,2},{4,5},{5,4},{6,7},{7,6},{8,9},{9,8},{10,11... | collective-permute-start | bytes 884744 | tf_op jit(solution)/shard_map/ppermute | solution.py:34
  336.7 9.9 %collective-permute-start.49 = (bf16[192,768]{1,0:T(8,128)(2,1)S(1)}, bf16[192,768]{1,0:T(8,128)(2,1)S(1)}, u32[]{:S(2)}, u32[]{:S(2)}) collective-permute-start(bf16[192,768]{1,0:T(8,128)(2,1)S(1)} %get-tuple-element.226), channel_id=1, source_target_pairs={{0,64},{64,0},{1,65},{65,1},{2,66},{66,2},{3,67},{67,3},{4,68},{68... | collective-permute-start | bytes 884744 | tf_op jit(solution)/shard_map/ppermute | solution.py:34
  341.5 20.9 %collective-permute-start.45 = (bf16[192,768]{1,0:T(8,128)(2,1)S(1)}, bf16[192,768]{1,0:T(8,128)(2,1)S(1)}, u32[]{:S(2)}, u32[]{:S(2)}) collective-permute-start(bf16[192,768]{1,0:T(8,128)(2,1)S(1)} %add_convert_fusion.8), channel_id=1, source_target_pairs={{0,64},{64,0},{1,65},{65,1},{2,66},{66,2},{3,67},{67,3},{4,68},{68... | collective-permute-start | bytes 884744 | tf_op jit(solution)/shard_map/ppermute | solution.py:34
  343.7 10.7 %collective-permute-start.48 = (bf16[192,768]{1,0:T(8,128)(2,1)S(1)}, bf16[192,768]{1,0:T(8,128)(2,1)S(1)}, u32[]{:S(2)}, u32[]{:S(2)}) collective-permute-start(bf16[192,768]{1,0:T(8,128)(2,1)S(1)} %add_convert_fusion.5), channel_id=1, source_target_pairs={{0,1},{1,0},{2,3},{3,2},{4,5},{5,4},{6,7},{7,6},{8,9},{9,8},{10,11... | collective-permute-start | bytes 884744 | tf_op jit(solution)/shard_map/ppermute | solution.py:34
  346.7 14.0 %collective-permute-start.50 = (bf16[192,768]{1,0:T(8,128)(2,1)S(1)}, bf16[192,768]{1,0:T(8,128)(2,1)S(1)}, u32[]{:S(2)}, u32[]{:S(2)}) collective-permute-start(bf16[192,768]{1,0:T(8,128)(2,1)S(1)} %add_convert_fusion.3), channel_id=1, source_target_pairs={{0,1},{1,0},{2,3},{3,2},{4,5},{5,4},{6,7},{7,6},{8,9},{9,8},{10,11... | collective-permute-start | bytes 884744 | tf_op jit(solution)/shard_map/ppermute | solution.py:34
  347.8 14.6 %collective-permute-start.46 = (bf16[192,768]{1,0:T(8,128)(2,1)S(1)}, bf16[192,768]{1,0:T(8,128)(2,1)S(1)}, u32[]{:S(2)}, u32[]{:S(2)}) collective-permute-start(bf16[192,768]{1,0:T(8,128)(2,1)S(1)} %add_convert_fusion.6), channel_id=1, source_target_pairs={{0,64},{64,0},{1,65},{65,1},{2,66},{66,2},{3,67},{67,3},{4,68},{68... | collective-permute-start | bytes 884744 | tf_op jit(solution)/shard_map/ppermute | solution.py:34
  354.4 23.2 %collective-permute-start.51 = (bf16[192,768]{1,0:T(8,128)(2,1)S(1)}, bf16[192,768]{1,0:T(8,128)(2,1)}, u32[]{:S(2)}, u32[]{:S(2)}) collective-permute-start(bf16[192,768]{1,0:T(8,128)(2,1)S(1)} %add_convert_fusion.4), channel_id=1, source_target_pairs={{0,64},{64,0},{1,65},{65,1},{2,66},{66,2},{3,67},{67,3},{4,68},{68... | collective-permute-start | bytes 884744 | tf_op jit(solution)/shard_map/ppermute | solution.py:34
  361.4 17.1 %collective-permute-start.52 = (bf16[192,768]{1,0:T(8,128)(2,1)}, bf16[192,768]{1,0:T(8,128)(2,1)}, u32[]{:S(2)}, u32[]{:S(2)}) collective-permute-start(bf16[192,768]{1,0:T(8,128)(2,1)} %add_convert_fusion.2), channel_id=1, source_target_pairs={{0,64},{64,0},{1,65},{65,1},{2,66},{66,2},{3,67},{67,3},{4,68},{68... | collective-permute-start | bytes 884744 | tf_op jit(solution)/shard_map/ppermute | solution.py:34
  385.4 12.7 %collective-permute-start.53 = (bf16[48,3072]{1,0:T(8,128)(2,1)S(1)}, bf16[48,3072]{1,0:T(8,128)(2,1)}, u32[]{:S(2)}, u32[]{:S(2)}) collective-permute-start(bf16[48,3072]{1,0:T(8,128)(2,1)S(1)} %broadcast_select_fusion.14), channel_id=1, source_target_pairs={{0,8},{8,0},{1,9},{9,1},{2,10},{10,2},{3,11},{11,3},{4,12},{12,4},... | collective-permute-start | bytes 884744 | tf_op jit(solution)/shard_map/ppermute | solution.py:34
  433.7 22.7 %copy-start.1 = (bf16[3,1,64,1536]{3,2,1,0:T(8,128)(2,1)S(1)}, bf16[3,1,64,1536]{3,2,1,0:T(8,128)(2,1)}, u32[]{:S(2)}) copy-start(bf16[3,1,64,1536]{3,2,1,0:T(8,128)(2,1)} %param.12) | copy-start | bytes 1769476
  435.1 12.3 %collective-permute-start.54 = (bf16[48,5376]{1,0:T(8,128)(2,1)S(1)}, bf16[48,5376]{1,0:T(8,128)(2,1)S(1)}, u32[]{:S(2)}, u32[]{:S(2)}) collective-permute-start(bf16[48,5376]{1,0:T(8,128)(2,1)S(1)} %get-tuple-element.262), channel_id=1, source_target_pairs={{0,8},{8,0},{1,9},{9,1},{2,10},{10,2},{3,11},{11,3},{4,12},{12,4},... | collective-permute-start | bytes 1548296 | tf_op jit(solution)/shard_map/ppermute | solution.py:34
  447.8 5.1 %collective-permute-start.56 = (bf16[48,4224]{1,0:T(8,128)(2,1)S(1)}, bf16[48,4224]{1,0:T(8,128)(2,1)S(1)}, u32[]{:S(2)}, u32[]{:S(2)}) collective-permute-start(bf16[48,4224]{1,0:T(8,128)(2,1)S(1)} %get-tuple-element.233), channel_id=1, source_target_pairs={{0,64},{64,0},{1,65},{65,1},{2,66},{66,2},{3,67},{67,3},{4,68},{68... | collective-permute-start | bytes 1216520 | tf_op jit(solution)/shard_map/ppermute | solution.py:34
  449.8 4.3 collective-permute-start.55
  454.2 1.7 collective-permute-start.57
  (29 other events, 210.8 us)
Sparse Core Ops, SparseCore 0:
  27.5 112.2 all-gather.2
  141.9 75.3 all-gather.4
  235.0 85.6 reduce-scatter.4
  325.2 108.5 reduce-scatter.2
where the time goes:
time: 472 us; the launch traced here: 463 us
  waiting for transfers between devices  213 us (45%)
  Pallas kernels  94 us (20%)
  starting transfers between devices  73.1 us (15%)
  local copies, waits for them, and re-layouts  49.6 us (11%)
  other arithmetic  19 us (4%)
  between operations  14.9 us (3%)
    ppermute x58, waiting for transfers between devices, swap(): return lax.ppermute(value, axis, [(0, 1), (1, 0)])  117 us
    ppermute x58, starting transfers between devices, swap(): return lax.ppermute(value, axis, [(0, 1), (1, 0)])  73 us
    all_gather x2, waiting for transfers between devices, gather_rows(): return lax.all_gather(pair, ('y', 'x'), axis=0, tiled=True)  61.3 us
    reduce_scatter x2, waiting for transfers between devices, scatter_pair(): return lax.psum_scatter(grad, ('y', 'x'), scatter_dimension=0, tiled=True)  34.6 us
    pallas_call x4, Pallas kernels, into_buffer(): pl.pallas_call(kernel, in_specs=specs, out_specs=[hbm_whole(), vmem_whole...  22.3 us
    pallas_call x5, Pallas kernels, fetch(): pl.pallas_call(functools.partial(fetch_kernel, column), in_specs=[hbm_who...  14.8 us
    pallas_call x2, Pallas kernels, attention_backward(): pl.pallas_call(functools.partial(attention_backward_kernel, rows // 128,...  12.2 us
  transfers between devices with their start and end apart: 62, of which 35 were waited for; matrix products, arithmetic and copies ran while one was open for 13% of the time, Pallas kernels for 17%

commit v1 on v0

--- a/solution.py
+++ b/solution.py
@@ -492,36 +492,46 @@
     )(core, x, *sums, hidden_grad, pair_weights, token)
 
 
-def mlp_in_kernel(core_ref, pair_grad_ref, w_any, _, *rest):
-    outs, w_ref, sems = rest[:-2], rest[-2], rest[-1]
-    copies = []
-    for which in (1, 0):
-        half = half_of(core_ref, which)
-        source = w_any.at[half, pl.ds(0, 2 * HIDDEN_COLS)]
-        copies.append(pltpu.make_async_copy(source, w_ref.at[half, :], sems.at[which]))
-        copies[-1].start()
-    for copy, which in zip(copies, (1, 0)):
+def mlp_in_kernel(core_ref, pair_grad_any, w_any, _, *rest):
+    outs, (pair_grad_ref, w_ref, sems) = rest[:-3], rest[-3:]
+    fetched = pltpu.make_async_copy(pair_grad_any, pair_grad_ref, sems.at[4])
+    fetched.start()
+    quarter = HALF // 2
+    pieces = []
+    for number, (which, part) in enumerate(((1, 0), (1, 1), (0, 0), (0, 1))):
+        position = core_ref[0] if which == 0 else 1 - core_ref[0]
+        features = pl.ds(pl.multiple_of(position * HALF + part * quarter, quarter), quarter)
+        source = w_any.at[features, pl.ds(0, 2 * HIDDEN_COLS)]
+        copy = pltpu.make_async_copy(source, w_ref.at[number], sems.at[number])
+        copy.start()
+        pieces.append((copy, which, slice(part * quarter, (part + 1) * quarter)))
+    fetched.wait()
+    for number, (copy, which, columns) in enumerate(pieces):
         copy.wait()
-        write_half(core_ref, which, pair_grad_ref, w_ref, slice(0, 2 * HIDDEN_COLS), outs)
+        product = nt_dot(pair_grad_ref[...], w_ref[number]).astype(BF16)
+        refs = outs[PARTS * which : PARTS * (which + 1)]
+        for at, ref in zip(row_parts(product.shape[0]), refs):
+            ref[:, columns] = product[at]
 
 
 def mlp_in(core, pair_grad, weights, token):
     rows = pair_grad.shape[0]
     return pl.pallas_call(
         mlp_in_kernel,
-        in_specs=[smem_whole(), vmem_whole()] + [hbm_whole()] * 2,
+        in_specs=[smem_whole()] + [hbm_whole()] * 3,
         out_specs=[vmem_whole()] * (2 * PARTS),
         out_shape=part_shapes(rows),
         scratch_shapes=[
-            pltpu.VMEM((WIDTH, 2 * HIDDEN_COLS), BF16),
-            pltpu.SemaphoreType.DMA((2,)),
+            pltpu.VMEM(pair_grad.shape, BF16),
+            pltpu.VMEM((4, HALF // 2, 2 * HIDDEN_COLS), BF16),
+            pltpu.SemaphoreType.DMA((5,)),
         ],
         compiler_params=params(18),
         cost_estimate=pl.CostEstimate(
             flops=4 * rows * WIDTH * HIDDEN_COLS, bytes_accessed=9_000_000, transcendentals=0
         ),
         name="mlp_in",
-    )(core, pair_grad, in_hbm(weights), token)
+    )(core, in_hbm(pair_grad), in_hbm(weights), token)
 
 
 def mlp_down_kernel(core_ref, hidden_ref, w_any, *rest):
@@ -747,14 +757,14 @@
     return totals + [swap(total, "section") for total in totals], beside
 
 
-def row_scales(gain_ref):
+def row_scales(gain_row):
     row = lax.broadcasted_iota(jnp.int32, (48, 48), 0)
     column = lax.broadcasted_iota(jnp.int32, (48, 48), 1)
-    return jnp.where(row == column, gain_ref[...].astype(F32), 0.0).astype(BF16)
+    return jnp.where(row == column, gain_row, 0.0).astype(BF16)
 
 
 def pack_kernel(core_ref, *rest):
-    sources, (mine_ref, give_ref), shards, sems = rest[:9], rest[9:11], rest[11:20], rest[20]
+    sources, (mine_ref, give_ref), shards, sems = rest[:8], rest[8:10], rest[10:18], rest[18]
     copies = [
         pltpu.make_async_copy(source, shard, sems.at[number])
         for number, (source, shard) in enumerate(zip(sources, shards))
@@ -762,13 +772,12 @@
     for copy in copies:
         copy.start()
     is_first = core_ref[0] == 0
-    (attn_gain_ref, mlp_gain_ref), shards = shards[:2], shards[2:]
-    for copy in copies[:2]:
-        copy.wait()
-    attn_scale, mlp_scale = row_scales(attn_gain_ref), row_scales(mlp_gain_ref)
+    gains_ref, shards = shards[0], shards[1:]
+    copies[0].wait()
+    attn_scale, mlp_scale = row_scales(gains_ref[0:1, :]), row_scales(gains_ref[1:2, :])
     start = 0
     for copy, shard, scale in zip(
-        copies[2:],
+        copies[1:],
         shards,
         (mlp_scale, mlp_scale, None, attn_scale, attn_scale, attn_scale, None),
     ):
@@ -909,7 +918,7 @@
 
     core_ref = core.astype(jnp.int32).reshape(1)
     mine, give = pack_shards(
-        core_ref, attn_gain, mlp_gain,
+        core_ref, jnp.concatenate([attn_gain, mlp_gain]).astype(F32),
         w_gate[0], w_up[0], w_down[0].T, w_query[0], key_weight[0], value_weight[0], w_out[0].T,
     )
     got = swap(give, "section")

time: 472 us -> 482 us (1.021)
  starting transfers between devices: 73.1 us -> 81.6 us
    ppermute x58, starting transfers between devices: 73 us -> 81.4 us  [swap(): return lax.ppermute(value, axis, [(0, 1), (1, 0)])]
where the time goes in v1:
time: 482 us; the launch traced here: 473 us
  waiting for transfers between devices  214 us (44%)
  Pallas kernels  94.1 us (20%)
  starting transfers between devices  81.6 us (17%)
  local copies, waits for them, and re-layouts  48.4 us (10%)
  other arithmetic  20.2 us (4%)
  between operations  15.1 us (3%)
    ppermute x58, waiting for transfers between devices, swap(): return lax.ppermute(value, axis, [(0, 1), (1, 0)])  117 us
    ppermute x58, starting transfers between devices, swap(): return lax.ppermute(value, axis, [(0, 1), (1, 0)])  81.4 us
    all_gather x2, waiting for transfers between devices, gather_rows(): return lax.all_gather(pair, ('y', 'x'), axis=0, tiled=True)  61.4 us
    reduce_scatter x2, waiting for transfers between devices, scatter_pair(): return lax.psum_scatter(grad, ('y', 'x'), scatter_dimension=0, tiled=True)  35.6 us
    pallas_call x4, Pallas kernels, into_buffer(): pl.pallas_call(kernel, in_specs=specs, out_specs=[hbm_whole(), vmem_whole...  22.2 us
    pallas_call x5, Pallas kernels, fetch(): pl.pallas_call(functools.partial(fetch_kernel, column), in_specs=[hbm_who...  14.7 us
    pallas_call x2, Pallas kernels, attention_backward(): pl.pallas_call(functools.partial(attention_backward_kernel, rows // 128,...  12.2 us
  transfers between devices with their start and end apart: 62, of which 35 were waited for; matrix products, arithmetic and copies ran while one was open for 13% of the time, Pallas kernels for 17%

profile of v1, /device:TPU:1, one launch (start us, length us, event | category | flops | bytes accessed | tf_op | source)
XLA Modules:
  0.0 473.3 jit_solution(9076690801603155137)
XLA Ops:
  8.5 2.1 pack_shards.1
  15.5 11.8 %collective-permute-done.3 = bf16[48,5376]{1,0:T(8,128)(2,1)S(1)} collective-permute-done((bf16[48,5376]{1,0:T(8,128)(2,1)S(1)}, bf16[48,5376]{1,0:T(8,128)(2,1)S(1)}, u32[]{:S(2)}, u32[]{:S(2)}) %collective-permute-start.3) | collective-permute-done | bytes 516128 | tf_op jit(solution)/shard_map/ppermute | solution.py:34
  29.9 6.4 %collective-permute-done.18 = bf16[48,3072]{1,0:T(8,128)(2,1)S(1)} collective-permute-done((bf16[48,3072]{1,0:T(8,128)(2,1)S(1)}, bf16[48,3072]{1,0:T(8,128)(2,1)S(1)}, u32[]{:S(2)}, u32[]{:S(2)}) %collective-permute-start.18) | collective-permute-done | bytes 294944 | tf_op jit(solution)/shard_map/ppermute | solution.py:34
  39.6 2.8 copy.31
  42.4 3.9 reshape.105
  46.3 2.9 collective-permute-start
  49.2 11.7 %collective-permute-done = bf16[3,64,1536]{2,1,0:T(8,128)(2,1)S(1)} collective-permute-done((bf16[3,64,1536]{2,1,0:T(8,128)(2,1)S(1)}, bf16[3,64,1536]{2,1,0:T(8,128)(2,1)S(1)}, u32[]{:S(2)}, u32[]{:S(2)}) %collective-permute-start) | collective-permute-done | bytes 589856 | tf_op jit(solution)/shard_map/ppermute | solution.py:34
  62.7 2.5 reshape.107
  65.2 4.2 copy.32
  69.4 3.9 reshape.108
  73.3 3.0 collective-permute-start.1
  76.3 10.7 %collective-permute-done.1 = bf16[3,64,1536]{2,1,0:T(8,128)(2,1)S(1)} collective-permute-done((bf16[3,64,1536]{2,1,0:T(8,128)(2,1)S(1)}, bf16[3,64,1536]{2,1,0:T(8,128)(2,1)S(1)}, u32[]{:S(2)}, u32[]{:S(2)}) %collective-permute-start.1) | collective-permute-done | bytes 589856 | tf_op jit(solution)/shard_map/ppermute | solution.py:34
  87.2 53.8 %all-gather.3.cloned.1.call-done.w_any = bf16[1536,5376]{1,0:T(8,128)(2,1)} async-done(((bf16[96,5376]{1,0:T(8,128)(2,1)}), bf16[1536,5376]{1,0:T(8,128)(2,1)}) %all-gather.3.cloned.1.call-update) | async-done | bytes 16515088 | tf_op jit(solution)/shard_map/all_gather | solution.py:873
  141.0 6.9 %attention_first.1 = (bf16[384,1536]{1,0:T(8,128)(2,1)}, bf16[384,768]{1,0:T(8,128)(2,1)}, f32[6,256,128]{2,1,0:T(8,128)}, bf16[384,384]{1,0:T(8,128)(2,1)S(1)},...) custom-call(s32[1]{0:T(128)} %bitcast.core_ref, ...), custom_call_target="tpu_custom_call" | custom-call | flops 1358954496 | bytes 8000000 | tf_op jit(solution)/shard_map/attention_first/pallas_call | solution.py:261
  150.0 2.9 collective-permute-start.5
  153.4 3.9 fetch.5
  157.3 2.5 collective-permute-done.5
  159.9 2.1 collective-permute-start.8
  162.0 4.2 collective-permute-done.7
  168.7 5.2 %mlp_forward.1 = (f32[384,1536]{1,0:T(8,128)}, bf16[384,1536]{1,0:T(8,128)(2,1)}, f32[384,1024]{1,0:T(8,128)}, f32[384,1024]{1,0:T(8,128)}, bf16[384,1024]{1,0:T...) custom-call(s32[1]{0:T(128)} %bitcast.core_ref, ...), custom_call_target="tpu_custom_call" | custom-call | flops 3623878656 | bytes 15000000 | tf_op jit(solution)/shard_map/mlp_forward/pallas_call | solution.py:367
  175.7 2.9 collective-permute-start.11
  179.1 2.2 fetch.6
  181.2 4.3 collective-permute-done.11
  185.6 2.1 collective-permute-start.14
  187.7 4.2 collective-permute-done.13
  194.4 4.9 %attention_next.1 = (bf16[384,1536]{1,0:T(8,128)(2,1)}, bf16[384,1536]{1,0:T(8,128)(2,1)}, bf16[384,768]{1,0:T(8,128)(2,1)}, f32[6,256,128]{2,1,0:T(8,128)}, bf1...) custom-call(s32[1]{0:T(128)} %bitcast.core_ref, ...), custom_call_target="tpu_custom_call" | custom-call | flops 1358954496 | bytes 8000000 | tf_op jit(solution)/shard_map/attention_next/pallas_call | solution.py:283
  201.0 2.9 collective-permute-start.17
  205.0 5.8 %collective-permute-done.17 = bf16[192,768]{1,0:T(8,128)(2,1)S(1)} collective-permute-done((bf16[192,768]{1,0:T(8,128)(2,1)S(1)}, bf16[192,768]{1,0:T(8,128)(2,1)S(1)}, u32[]{:S(2)}, u32[]{:S(2)}) %collective-permute-start.17) | collective-permute-done | bytes 294944 | tf_op jit(solution)/shard_map/ppermute | solution.py:34
  210.9 7.6 %all-gather.5.cloned.1.call-done.w_any = bf16[1536,3072]{1,0:T(8,128)(2,1)} async-done(((bf16[96,3072]{1,0:T(8,128)(2,1)}), bf16[1536,3072]{1,0:T(8,128)(2,1)}) %all-gather.5.cloned.1.call-update) | async-done | bytes 9437200 | tf_op jit(solution)/shard_map/all_gather | solution.py:873
  220.3 8.8 %collective-permute-start.22 = (bf16[192,768]{1,0:T(8,128)(2,1)S(1)}, bf16[192,768]{1,0:T(8,128)(2,1)S(1)}, u32[]{:S(2)}, u32[]{:S(2)}) collective-permute-start(bf16[192,768]{1,0:T(8,128)(2,1)S(1)} %add_convert_fusion.22.rest_1_), channel_id=1, source_target_pairs={{0,64},{64,0},{1,65},{65,1},{2,66},{66,2},{3,67},{67,3},{4,68},{68... | collective-permute-start | bytes 884744 | tf_op jit(solution)/shard_map/ppermute | solution.py:34
  229.1 3.8 mlp_ahead.1
  232.9 4.5 mlp_last.1
  237.5 7.1 %mlp_weights.2 = (bf16[1536,3072]{1,0:T(8,128)(2,1)}, f32[8,128]{1,0:T(8,128)S(1)}) custom-call(bf16[384,1536]{1,0:T(8,128)(2,1)S(1)} %get-tuple-element.163.second_ref, bf16[384,1536]{1,0:T(8,128)(2,1)S(1)} %bitcast.52, bf16[384,2048]{1,0:T(8,128)(2,1)S(1)} %get-tuple-element.162.pair_grad_ref.pair_grad_any, bf16[384,1024]{1,0:T(8,128)(2,1)S(1)} %get-tuple-element.164.hidden_ref), custom_call_target="tpu_custom_call" | custom-call | flops 3623878656 | bytes 14495514 | tf_op jit(solution)/shard_map/mlp_weights/pallas_call | solution.py:691
  244.7 6.0 %mlp_in.1 = (bf16[192,768]{1,0:T(8,128)(2,1)S(1)}, bf16[192,768]{1,0:T(8,128)(2,1)S(1)}, bf16[192,768]{1,0:T(8,128)(2,1)S(1)}, bf16[192,768]{1,0:T(8,128)(2,1)S(1)}) custom-call(s32[1]{0:T(128)} %bitcast.core_ref, bf16[384,2048]{1,0:T(8,128)(2,1)} %copy-done.15, bf16[1536,3072]{1,0:T(8,128)(2,1)} %all-gather.5.cloned.1.call-done.w_any, ...), custom_call_target="tpu_custom_call" | custom-call | flops 2415919104 | bytes 9000000 | tf_op jit(solution)/shard_map/mlp_in/pallas_call | solution.py:519
  252.5 2.9 collective-permute-start.24
  255.9 2.2 fetch.7
  258.0 4.3 collective-permute-done.24
  264.5 4.2 collective-permute-done.26
  271.6 5.8 %attention_backward.2 = (f32[384,1536]{1,0:T(8,128)S(1)}, bf16[384,1536]{1,0:T(8,128)(2,1)S(1)}, bf16[384,768]{1,0:T(8,128)(2,1)S(1)}, bf16[192,768]{1,0:T(8,128...) custom-call(s32[1]{0:T(128)} %bitcast.core_ref, ...), custom_call_target="tpu_custom_call" | custom-call | flops 1358954496 | bytes 8000000 | tf_op jit(solution)/shard_map/attention_backward/pallas_call | solution.py:637
  279.2 2.9 collective-permute-start.30
  282.6 4.0 attention_weights.2
  286.6 4.3 fetch.8
  291.5 3.8 collective-permute-done.32
  297.9 5.4 %mlp_backward.1 = (bf16[384,1536]{1,0:T(8,128)(2,1)S(1)}, bf16[384,2048]{1,0:T(8,128)(2,1)S(1)}, bf16[192,768]{1,0:T(8,128)(2,1)S(1)}, bf16[192,768]{1,0:T(8,128...) custom-call(s32[1]{0:T(128)} %bitcast.core_ref, bf16[384,1536]{1,0:T(8,128)(2,1)S(1)} %copy-done.9, ...), custom_call_target="tpu_custom_call" | custom-call | flops 3623878656 | bytes 15000000 | tf_op jit(solution)/shard_map/mlp_backward/pallas_call | solution.py:408
  305.2 2.9 collective-permute-start.36
  308.6 7.6 %mlp_weights.3 = (bf16[1536,5376]{1,0:T(8,128)(2,1)}, f32[8,128]{1,0:T(8,128)}) custom-call(bf16[384,1536]{1,0:T(8,128)(2,1)S(1)} %copy-done.17, bf16[384,1536]{1,0:T(8,128)(2,1)S(1)} %get-tuple-element.193.g_ref, bf16[384,2048]{1,0:T(8,128)(2,1)S(1)} %get-tuple-element.201.pair_grad_ref, ...), custom_call_target="tpu_custom_call", output_to_operand_aliasing={{0}: (4, {})} | custom-call | flops 3623878656 | bytes 14495514 | tf_op jit(solution)/shard_map/mlp_weights/pallas_call | solution.py:691
  316.3 2.2 fetch.9
  323.9 6.3 %attention_backward.3 = (f32[384,1536]{1,0:T(8,128)}, bf16[384,1536]{1,0:T(8,128)(2,1)S(1)}, bf16[384,768]{1,0:T(8,128)(2,1)S(1)}) custom-call(s32[1]{0:T(128)} %bitcast.core_ref, bf16[384,1536]{1,0:T(8,128)(2,1)S(1)} %get-tuple-element.193.g_ref, f32[384,1536]{1,0:T(8,128)S(1)} %copy-done.5, bf16[192,768]{1,0:T(8,128)(2,1)S(1)} %add_convert_fusion.12.rest_0_, ...), custom_call_target="tpu_custom_call" | custom-call | flops 1358954496 | bytes 8000000 | tf_op jit(solution)/shard_map/attention_backward/pallas_call | solution.py:637
  330.3 3.5 attention_weights.3
  334.9 3.5 mlp_down.1
  340.4 2.9 collective-permute-start.42
  345.8 4.4 collective-permute-done.42
  352.4 2.9 collective-permute-start.48
  358.4 4.7 %collective-permute-done.48 = bf16[192,768]{1,0:T(8,128)(2,1)S(1)} collective-permute-done((bf16[192,768]{1,0:T(8,128)(2,1)S(1)}, bf16[192,768]{1,0:T(8,128)(2,1)S(1)}, u32[]{:S(2)}, u32[]{:S(2)}) %collective-permute-start.48) | collective-permute-done | bytes 294944 | tf_op jit(solution)/shard_map/ppermute | solution.py:34
  364.7 4.7 %collective-permute-done.50 = bf16[192,768]{1,0:T(8,128)(2,1)S(1)} collective-permute-done((bf16[192,768]{1,0:T(8,128)(2,1)S(1)}, bf16[192,768]{1,0:T(8,128)(2,1)S(1)}, u32[]{:S(2)}, u32[]{:S(2)}) %collective-permute-start.50) | collective-permute-done | bytes 294944 | tf_op jit(solution)/shard_map/ppermute | solution.py:34
  375.1 3.4 reshape.112
  378.5 3.4 copy.33
  381.9 4.6 reshape.113
  395.8 2.2 fusion.6
  398.0 2.6 reshape.116
  402.3 4.7 reshape.117
  408.0 35.6 %reduce-scatter.3.cloned.1.call-done = bf16[96,5376]{1,0:T(8,128)(2,1)} async-done(((bf16[1536,5376]{1,0:T(8,128)(2,1)}), bf16[96,5376]{1,0:T(8,128)(2,1)}) %reduce-scatter.3.cloned.1.call-update) | async-done | bytes 1032208 | tf_op jit(solution)/shard_map/reduce_scatter | solution.py:877
  446.4 10.9 %collective-permute-done.54.arrived_ref = bf16[48,5376]{1,0:T(8,128)(2,1)S(1)} collective-permute-done((bf16[48,5376]{1,0:T(8,128)(2,1)S(1)}, bf16[48,5376]{1,0:T(8,128)(2,1)S(1)}, u32[]{:S(2)}, u32[]{:S(2)}) %collective-permute-start.54) | collective-permute-done | bytes 516128 | tf_op jit(solution)/shard_map/ppermute | solution.py:34
  459.7 3.0 collective-permute-start.55
  (233 shorter events, 88.0 us)
Async XLA Ops:
  7.2 30.2 %copy-start = (bf16[3,1,64,1536]{3,2,1,0:T(8,128)(2,1)S(1)}, bf16[3,1,64,1536]{3,2,1,0:T(8,128)(2,1)}, u32[]{:S(2)}) copy-start(bf16[3,1,64,1536]{3,2,1,0:T(8,128)(2,1)} %param.12) | copy-start | bytes 1769476
  7.2 133.8 %all-gather.3.cloned.1.call-start = ((), (), s32[]{:S(2)}) async-start(), calls=%async_computation.2 | async-start | bytes 17547264 | tf_op jit(solution)/shard_map/all_gather | solution.py:873
  10.7 2.9 collective-permute-start.2
  13.7 13.6 %collective-permute-start.3 = (bf16[48,5376]{1,0:T(8,128)(2,1)S(1)}, bf16[48,5376]{1,0:T(8,128)(2,1)S(1)}, u32[]{:S(2)}, u32[]{:S(2)}) collective-permute-start(bf16[48,5376]{1,0:T(8,128)(2,1)S(1)} %pad_maximum_fusion.7), channel_id=1, source_target_pairs={{0,8},{8,0},{1,9},{9,1},{2,10},{10,2},{3,11},{11,3},{4,12},{12,4},... | collective-permute-start | bytes 1548296 | tf_op jit(solution)/shard_map/ppermute | solution.py:34
  28.6 189.9 %all-gather.5.cloned.1.call-start = ((), (), s32[]{:S(2)}) async-start(), calls=%async_computation.3 | async-start | bytes 10027008 | tf_op jit(solution)/shard_map/all_gather | solution.py:873
  28.7 7.7 %collective-permute-start.18 = (bf16[48,3072]{1,0:T(8,128)(2,1)S(1)}, bf16[48,3072]{1,0:T(8,128)(2,1)S(1)}, u32[]{:S(2)}, u32[]{:S(2)}) collective-permute-start(bf16[48,3072]{1,0:T(8,128)(2,1)S(1)} %slice.83), channel_id=1, source_target_pairs={{0,8},{8,0},{1,9},{9,1},{2,10},{10,2},{3,11},{11,3},{4,12},{12,4},... | collective-permute-start | bytes 884744 | tf_op jit(solution)/shard_map/ppermute | solution.py:34
  37.3 355.8 %reduce-scatter.5.cloned.1.call-start = ((), (), s32[]{:S(2)}) async-start(), calls=%async_computation.5 | async-start | bytes 10027008 | tf_op jit(solution)/shard_map/reduce_scatter | solution.py:877
  46.3 14.6 %collective-permute-start = (bf16[3,64,1536]{2,1,0:T(8,128)(2,1)S(1)}, bf16[3,64,1536]{2,1,0:T(8,128)(2,1)S(1)}, u32[]{:S(2)}, u32[]{:S(2)}) collective-permute-start(bf16[3,64,1536]{2,1,0:T(8,128)(2,1)S(1)} %reshape.105), channel_id=1, source_target_pairs={{0,1},{1,0},{2,3},{3,2},{4,5},{5,4},{6,7},{7,6},{8,9},{9,8},{10,11... | collective-permute-start | bytes 1769480 | tf_op jit(solution)/shard_map/ppermute | solution.py:34
  73.3 13.7 %collective-permute-start.1 = (bf16[3,64,1536]{2,1,0:T(8,128)(2,1)S(1)}, bf16[3,64,1536]{2,1,0:T(8,128)(2,1)S(1)}, u32[]{:S(2)}, u32[]{:S(2)}) collective-permute-start(bf16[3,64,1536]{2,1,0:T(8,128)(2,1)S(1)} %reshape.108), channel_id=1, source_target_pairs={{0,1},{1,0},{2,3},{3,2},{4,5},{5,4},{6,7},{7,6},{8,9},{9,8},{10,11... | collective-permute-start | bytes 1769480 | tf_op jit(solution)/shard_map/ppermute | solution.py:34
  147.9 2.0 collective-permute-start.4
  148.7 4.2 collective-permute-start.6
  150.0 9.8 %collective-permute-start.5 = (bf16[192,768]{1,0:T(8,128)(2,1)S(1)}, bf16[192,768]{1,0:T(8,128)(2,1)S(1)}, u32[]{:S(2)}, u32[]{:S(2)}) collective-permute-start(bf16[192,768]{1,0:T(8,128)(2,1)S(1)} %add_convert_fusion.33), channel_id=1, source_target_pairs={{0,1},{1,0},{2,3},{3,2},{4,5},{5,4},{6,7},{7,6},{8,9},{9,8},{10,11... | collective-permute-start | bytes 884744 | tf_op jit(solution)/shard_map/ppermute | solution.py:34
  153.1 13.1 %collective-permute-start.7 = (bf16[192,768]{1,0:T(8,128)(2,1)S(1)}, bf16[192,768]{1,0:T(8,128)(2,1)S(1)}, u32[]{:S(2)}, u32[]{:S(2)}) collective-permute-start(bf16[192,768]{1,0:T(8,128)(2,1)S(1)} %add_convert_fusion.31), channel_id=1, source_target_pairs={{0,1},{1,0},{2,3},{3,2},{4,5},{5,4},{6,7},{7,6},{8,9},{9,8},{10,11... | collective-permute-start | bytes 884744 | tf_op jit(solution)/shard_map/ppermute | solution.py:34
  159.9 7.6 %collective-permute-start.8 = (bf16[192,768]{1,0:T(8,128)(2,1)S(1)}, bf16[192,768]{1,0:T(8,128)(2,1)S(1)}, u32[]{:S(2)}, u32[]{:S(2)}) collective-permute-start(bf16[192,768]{1,0:T(8,128)(2,1)S(1)} %add_convert_fusion.32.rest_0_), channel_id=1, source_target_pairs={{0,64},{64,0},{1,65},{65,1},{2,66},{66,2},{3,67},{67,3},{4,68},{68... | collective-permute-start | bytes 884744 | tf_op jit(solution)/shard_map/ppermute | solution.py:34
  166.2 2.5 collective-permute-start.9
  174.0 1.7 collective-permute-start.10
  174.4 4.2 collective-permute-start.12
  175.7 9.8 %collective-permute-start.11 = (bf16[192,768]{1,0:T(8,128)(2,1)S(1)}, bf16[192,768]{1,0:T(8,128)(2,1)S(1)}, u32[]{:S(2)}, u32[]{:S(2)}) collective-permute-start(bf16[192,768]{1,0:T(8,128)(2,1)S(1)} %add_convert_fusion.29), channel_id=1, source_target_pairs={{0,1},{1,0},{2,3},{3,2},{4,5},{5,4},{6,7},{7,6},{8,9},{9,8},{10,11... | collective-permute-start | bytes 884744 | tf_op jit(solution)/shard_map/ppermute | solution.py:34
  178.7 13.1 %collective-permute-start.13 = (bf16[192,768]{1,0:T(8,128)(2,1)S(1)}, bf16[192,768]{1,0:T(8,128)(2,1)S(1)}, u32[]{:S(2)}, u32[]{:S(2)}) collective-permute-start(bf16[192,768]{1,0:T(8,128)(2,1)S(1)} %add_convert_fusion.27), channel_id=1, source_target_pairs={{0,1},{1,0},{2,3},{3,2},{4,5},{5,4},{6,7},{7,6},{8,9},{9,8},{10,11... | collective-permute-start | bytes 884744 | tf_op jit(solution)/shard_map/ppermute | solution.py:34
  185.6 7.6 %collective-permute-start.14 = (bf16[192,768]{1,0:T(8,128)(2,1)S(1)}, bf16[192,768]{1,0:T(8,128)(2,1)S(1)}, u32[]{:S(2)}, u32[]{:S(2)}) collective-permute-start(bf16[192,768]{1,0:T(8,128)(2,1)S(1)} %add_convert_fusion.28.rest_0_), channel_id=1, source_target_pairs={{0,64},{64,0},{1,65},{65,1},{2,66},{66,2},{3,67},{67,3},{4,68},{68... | collective-permute-start | bytes 884744 | tf_op jit(solution)/shard_map/ppermute | solution.py:34
  191.9 2.5 collective-permute-start.15
  199.3 1.7 collective-permute-start.16
  199.7 4.3 collective-permute-start.19
  201.0 9.8 %collective-permute-start.17 = (bf16[192,768]{1,0:T(8,128)(2,1)S(1)}, bf16[192,768]{1,0:T(8,128)(2,1)S(1)}, u32[]{:S(2)}, u32[]{:S(2)}) collective-permute-start(bf16[192,768]{1,0:T(8,128)(2,1)S(1)} %add_convert_fusion.25), channel_id=1, source_target_pairs={{0,1},{1,0},{2,3},{3,2},{4,5},{5,4},{6,7},{7,6},{8,9},{9,8},{10,11... | collective-permute-start | bytes 884744 | tf_op jit(solution)/shard_map/ppermute | solution.py:34
  204.8 14.4 %collective-permute-start.20 = (bf16[192,768]{1,0:T(8,128)(2,1)}, bf16[192,768]{1,0:T(8,128)(2,1)}, u32[]{:S(2)}, u32[]{:S(2)}) collective-permute-start(bf16[192,768]{1,0:T(8,128)(2,1)} %add_convert_fusion.23), channel_id=1, source_target_pairs={{0,1},{1,0},{2,3},{3,2},{4,5},{5,4},{6,7},{7,6},{8,9},{9,8},{10,11... | collective-permute-start | bytes 884744 | tf_op jit(solution)/shard_map/ppermute | solution.py:34
  218.5 14.4 %collective-permute-start.21 = (bf16[192,768]{1,0:T(8,128)(2,1)S(1)}, bf16[192,768]{1,0:T(8,128)(2,1)S(1)}, u32[]{:S(2)}, u32[]{:S(2)}) collective-permute-start(bf16[192,768]{1,0:T(8,128)(2,1)S(1)} %add_convert_fusion.24.rest_0_), channel_id=1, source_target_pairs={{0,64},{64,0},{1,65},{65,1},{2,66},{66,2},{3,67},{67,3},{4,68},{68... | collective-permute-start | bytes 884744 | tf_op jit(solution)/shard_map/ppermute | solution.py:34
  220.3 12.6 %collective-permute-start.22 = (bf16[192,768]{1,0:T(8,128)(2,1)S(1)}, bf16[192,768]{1,0:T(8,128)(2,1)S(1)}, u32[]{:S(2)}, u32[]{:S(2)}) collective-permute-start(bf16[192,768]{1,0:T(8,128)(2,1)S(1)} %add_convert_fusion.22.rest_1_), channel_id=1, source_target_pairs={{0,64},{64,0},{1,65},{65,1},{2,66},{66,2},{3,67},{67,3},{4,68},{68... | collective-permute-start | bytes 884744 | tf_op jit(solution)/shard_map/ppermute | solution.py:34
  244.6 199.0 %reduce-scatter.3.cloned.1.call-start = ((), (), s32[]{:S(2)}) async-start(), calls=%async_computation.4 | async-start | bytes 17547264 | tf_op jit(solution)/shard_map/reduce_scatter | solution.py:877
  250.6 1.8 collective-permute-start.23
  251.2 4.2 collective-permute-start.25
  252.5 9.8 %collective-permute-start.24 = (bf16[192,768]{1,0:T(8,128)(2,1)S(1)}, bf16[192,768]{1,0:T(8,128)(2,1)S(1)}, u32[]{:S(2)}, u32[]{:S(2)}) collective-permute-start(bf16[192,768]{1,0:T(8,128)(2,1)S(1)} %add_convert_fusion.21), channel_id=1, source_target_pairs={{0,1},{1,0},{2,3},{3,2},{4,5},{5,4},{6,7},{7,6},{8,9},{9,8},{10,11... | collective-permute-start | bytes 884744 | tf_op jit(solution)/shard_map/ppermute | solution.py:34
  255.5 13.1 %collective-permute-start.26 = (bf16[192,768]{1,0:T(8,128)(2,1)S(1)}, bf16[192,768]{1,0:T(8,128)(2,1)S(1)}, u32[]{:S(2)}, u32[]{:S(2)}) collective-permute-start(bf16[192,768]{1,0:T(8,128)(2,1)S(1)} %add_convert_fusion.19), channel_id=1, source_target_pairs={{0,1},{1,0},{2,3},{3,2},{4,5},{5,4},{6,7},{7,6},{8,9},{9,8},{10,11... | collective-permute-start | bytes 884744 | tf_op jit(solution)/shard_map/ppermute | solution.py:34
  262.4 8.0 %collective-permute-start.27 = (bf16[192,768]{1,0:T(8,128)(2,1)S(1)}, bf16[192,768]{1,0:T(8,128)(2,1)S(1)}, u32[]{:S(2)}, u32[]{:S(2)}) collective-permute-start(bf16[192,768]{1,0:T(8,128)(2,1)S(1)} %add_convert_fusion.20.rest_0_), channel_id=1, source_target_pairs={{0,64},{64,0},{1,65},{65,1},{2,66},{66,2},{3,67},{67,3},{4,68},{68... | collective-permute-start | bytes 884744 | tf_op jit(solution)/shard_map/ppermute | solution.py:34
  268.7 2.9 collective-permute-start.28
  277.5 1.7 collective-permute-start.29
  277.9 4.2 collective-permute-start.31
  279.2 11.8 %collective-permute-start.30 = (bf16[192,768]{1,0:T(8,128)(2,1)S(1)}, bf16[192,768]{1,0:T(8,128)(2,1)S(1)}, u32[]{:S(2)}, u32[]{:S(2)}) collective-permute-start(bf16[192,768]{1,0:T(8,128)(2,1)S(1)} %add_convert_fusion.17), channel_id=1, source_target_pairs={{0,1},{1,0},{2,3},{3,2},{4,5},{5,4},{6,7},{7,6},{8,9},{9,8},{10,11... | collective-permute-start | bytes 884744 | tf_op jit(solution)/shard_map/ppermute | solution.py:34
  282.2 13.1 %collective-permute-start.32 = (bf16[192,768]{1,0:T(8,128)(2,1)S(1)}, bf16[192,768]{1,0:T(8,128)(2,1)S(1)}, u32[]{:S(2)}, u32[]{:S(2)}) collective-permute-start(bf16[192,768]{1,0:T(8,128)(2,1)S(1)} %add_convert_fusion.15), channel_id=1, source_target_pairs={{0,1},{1,0},{2,3},{3,2},{4,5},{5,4},{6,7},{7,6},{8,9},{9,8},{10,11... | collective-permute-start | bytes 884744 | tf_op jit(solution)/shard_map/ppermute | solution.py:34
  291.1 5.6 %collective-permute-start.33 = (bf16[192,768]{1,0:T(8,128)(2,1)S(1)}, bf16[192,768]{1,0:T(8,128)(2,1)S(1)}, u32[]{:S(2)}, u32[]{:S(2)}) collective-permute-start(bf16[192,768]{1,0:T(8,128)(2,1)S(1)} %add_convert_fusion.16.rest_0_), channel_id=1, source_target_pairs={{0,64},{64,0},{1,65},{65,1},{2,66},{66,2},{3,67},{67,3},{4,68},{68... | collective-permute-start | bytes 884744 | tf_op jit(solution)/shard_map/ppermute | solution.py:34
  295.4 2.5 collective-permute-start.34
  303.3 1.8 collective-permute-start.35
  303.9 4.2 collective-permute-start.37
  305.2 13.2 %collective-permute-start.36 = (bf16[192,768]{1,0:T(8,128)(2,1)S(1)}, bf16[192,768]{1,0:T(8,128)(2,1)S(1)}, u32[]{:S(2)}, u32[]{:S(2)}) collective-permute-start(bf16[192,768]{1,0:T(8,128)(2,1)S(1)} %add_convert_fusion.13), channel_id=1, source_target_pairs={{0,1},{1,0},{2,3},{3,2},{4,5},{5,4},{6,7},{7,6},{8,9},{9,8},{10,11... | collective-permute-start | bytes 884744 | tf_op jit(solution)/shard_map/ppermute | solution.py:34
  308.2 13.1 %collective-permute-start.38 = (bf16[192,768]{1,0:T(8,128)(2,1)S(1)}, bf16[192,768]{1,0:T(8,128)(2,1)S(1)}, u32[]{:S(2)}, u32[]{:S(2)}) collective-permute-start(bf16[192,768]{1,0:T(8,128)(2,1)S(1)} %add_convert_fusion.11), channel_id=1, source_target_pairs={{0,1},{1,0},{2,3},{3,2},{4,5},{5,4},{6,7},{7,6},{8,9},{9,8},{10,11... | collective-permute-start | bytes 884744 | tf_op jit(solution)/shard_map/ppermute | solution.py:34
  318.5 4.2 collective-permute-start.39
  321.4 2.5 collective-permute-start.40
  338.4 1.9 collective-permute-start.41
  339.4 5.8 %collective-permute-start.43 = (bf16[192,768]{1,0:T(8,128)(2,1)S(1)}, bf16[192,768]{1,0:T(8,128)(2,1)S(1)}, u32[]{:S(2)}, u32[]{:S(2)}) collective-permute-start(bf16[192,768]{1,0:T(8,128)(2,1)S(1)} %get-tuple-element.220), channel_id=1, source_target_pairs={{0,64},{64,0},{1,65},{65,1},{2,66},{66,2},{3,67},{67,3},{4,68},{68... | collective-permute-start | bytes 884744 | tf_op jit(solution)/shard_map/ppermute | solution.py:34
  340.4 9.8 %collective-permute-start.42 = (bf16[192,768]{1,0:T(8,128)(2,1)S(1)}, bf16[192,768]{1,0:T(8,128)(2,1)S(1)}, u32[]{:S(2)}, u32[]{:S(2)}) collective-permute-start(bf16[192,768]{1,0:T(8,128)(2,1)S(1)} %add_convert_fusion.9), channel_id=1, source_target_pairs={{0,1},{1,0},{2,3},{3,2},{4,5},{5,4},{6,7},{7,6},{8,9},{9,8},{10,11... | collective-permute-start | bytes 884744 | tf_op jit(solution)/shard_map/ppermute | solution.py:34
  344.5 7.9 %collective-permute-start.47 = (bf16[192,768]{1,0:T(8,128)(2,1)S(1)}, bf16[192,768]{1,0:T(8,128)(2,1)S(1)}, u32[]{:S(2)}, u32[]{:S(2)}) collective-permute-start(bf16[192,768]{1,0:T(8,128)(2,1)S(1)} %get-tuple-element.224), channel_id=1, source_target_pairs={{0,64},{64,0},{1,65},{65,1},{2,66},{66,2},{3,67},{67,3},{4,68},{68... | collective-permute-start | bytes 884744 | tf_op jit(solution)/shard_map/ppermute | solution.py:34
  345.3 11.2 %collective-permute-start.44 = (bf16[192,768]{1,0:T(8,128)(2,1)S(1)}, bf16[192,768]{1,0:T(8,128)(2,1)S(1)}, u32[]{:S(2)}, u32[]{:S(2)}) collective-permute-start(bf16[192,768]{1,0:T(8,128)(2,1)S(1)} %add_convert_fusion.7), channel_id=1, source_target_pairs={{0,1},{1,0},{2,3},{3,2},{4,5},{5,4},{6,7},{7,6},{8,9},{9,8},{10,11... | collective-permute-start | bytes 884744 | tf_op jit(solution)/shard_map/ppermute | solution.py:34
  345.5 9.9 %collective-permute-start.49 = (bf16[192,768]{1,0:T(8,128)(2,1)S(1)}, bf16[192,768]{1,0:T(8,128)(2,1)S(1)}, u32[]{:S(2)}, u32[]{:S(2)}) collective-permute-start(bf16[192,768]{1,0:T(8,128)(2,1)S(1)} %get-tuple-element.226), channel_id=1, source_target_pairs={{0,64},{64,0},{1,65},{65,1},{2,66},{66,2},{3,67},{67,3},{4,68},{68... | collective-permute-start | bytes 884744 | tf_op jit(solution)/shard_map/ppermute | solution.py:34
  350.3 20.9 %collective-permute-start.45 = (bf16[192,768]{1,0:T(8,128)(2,1)S(1)}, bf16[192,768]{1,0:T(8,128)(2,1)S(1)}, u32[]{:S(2)}, u32[]{:S(2)}) collective-permute-start(bf16[192,768]{1,0:T(8,128)(2,1)S(1)} %add_convert_fusion.8), channel_id=1, source_target_pairs={{0,64},{64,0},{1,65},{65,1},{2,66},{66,2},{3,67},{67,3},{4,68},{68... | collective-permute-start | bytes 884744 | tf_op jit(solution)/shard_map/ppermute | solution.py:34
  352.4 10.7 %collective-permute-start.48 = (bf16[192,768]{1,0:T(8,128)(2,1)S(1)}, bf16[192,768]{1,0:T(8,128)(2,1)S(1)}, u32[]{:S(2)}, u32[]{:S(2)}) collective-permute-start(bf16[192,768]{1,0:T(8,128)(2,1)S(1)} %add_convert_fusion.5), channel_id=1, source_target_pairs={{0,1},{1,0},{2,3},{3,2},{4,5},{5,4},{6,7},{7,6},{8,9},{9,8},{10,11... | collective-permute-start | bytes 884744 | tf_op jit(solution)/shard_map/ppermute | solution.py:34
  355.5 14.0 %collective-permute-start.50 = (bf16[192,768]{1,0:T(8,128)(2,1)S(1)}, bf16[192,768]{1,0:T(8,128)(2,1)S(1)}, u32[]{:S(2)}, u32[]{:S(2)}) collective-permute-start(bf16[192,768]{1,0:T(8,128)(2,1)S(1)} %add_convert_fusion.3), channel_id=1, source_target_pairs={{0,1},{1,0},{2,3},{3,2},{4,5},{5,4},{6,7},{7,6},{8,9},{9,8},{10,11... | collective-permute-start | bytes 884744 | tf_op jit(solution)/shard_map/ppermute | solution.py:34
  356.6 14.6 %collective-permute-start.46 = (bf16[192,768]{1,0:T(8,128)(2,1)S(1)}, bf16[192,768]{1,0:T(8,128)(2,1)S(1)}, u32[]{:S(2)}, u32[]{:S(2)}) collective-permute-start(bf16[192,768]{1,0:T(8,128)(2,1)S(1)} %add_convert_fusion.6), channel_id=1, source_target_pairs={{0,64},{64,0},{1,65},{65,1},{2,66},{66,2},{3,67},{67,3},{4,68},{68... | collective-permute-start | bytes 884744 | tf_op jit(solution)/shard_map/ppermute | solution.py:34
  363.2 23.3 %collective-permute-start.51 = (bf16[192,768]{1,0:T(8,128)(2,1)S(1)}, bf16[192,768]{1,0:T(8,128)(2,1)}, u32[]{:S(2)}, u32[]{:S(2)}) collective-permute-start(bf16[192,768]{1,0:T(8,128)(2,1)S(1)} %add_convert_fusion.4), channel_id=1, source_target_pairs={{0,64},{64,0},{1,65},{65,1},{2,66},{66,2},{3,67},{67,3},{4,68},{68... | collective-permute-start | bytes 884744 | tf_op jit(solution)/shard_map/ppermute | solution.py:34
  370.2 17.3 %collective-permute-start.52 = (bf16[192,768]{1,0:T(8,128)(2,1)}, bf16[192,768]{1,0:T(8,128)(2,1)}, u32[]{:S(2)}, u32[]{:S(2)}) collective-permute-start(bf16[192,768]{1,0:T(8,128)(2,1)} %add_convert_fusion.2), channel_id=1, source_target_pairs={{0,64},{64,0},{1,65},{65,1},{2,66},{66,2},{3,67},{67,3},{4,68},{68... | collective-permute-start | bytes 884744 | tf_op jit(solution)/shard_map/ppermute | solution.py:34
  394.2 12.7 %collective-permute-start.53 = (bf16[48,3072]{1,0:T(8,128)(2,1)S(1)}, bf16[48,3072]{1,0:T(8,128)(2,1)}, u32[]{:S(2)}, u32[]{:S(2)}) collective-permute-start(bf16[48,3072]{1,0:T(8,128)(2,1)S(1)} %broadcast_select_fusion.14), channel_id=1, source_target_pairs={{0,8},{8,0},{1,9},{9,1},{2,10},{10,2},{3,11},{11,3},{4,12},{12,4},... | collective-permute-start | bytes 884744 | tf_op jit(solution)/shard_map/ppermute | solution.py:34
  443.6 22.7 %copy-start.1 = (bf16[3,1,64,1536]{3,2,1,0:T(8,128)(2,1)S(1)}, bf16[3,1,64,1536]{3,2,1,0:T(8,128)(2,1)}, u32[]{:S(2)}) copy-start(bf16[3,1,64,1536]{3,2,1,0:T(8,128)(2,1)} %param.12) | copy-start | bytes 1769476
  445.0 12.3 %collective-permute-start.54 = (bf16[48,5376]{1,0:T(8,128)(2,1)S(1)}, bf16[48,5376]{1,0:T(8,128)(2,1)S(1)}, u32[]{:S(2)}, u32[]{:S(2)}) collective-permute-start(bf16[48,5376]{1,0:T(8,128)(2,1)S(1)} %get-tuple-element.262), channel_id=1, source_target_pairs={{0,8},{8,0},{1,9},{9,1},{2,10},{10,2},{3,11},{11,3},{4,12},{12,4},... | collective-permute-start | bytes 1548296 | tf_op jit(solution)/shard_map/ppermute | solution.py:34
  457.6 5.3 %collective-permute-start.56 = (bf16[48,4224]{1,0:T(8,128)(2,1)S(1)}, bf16[48,4224]{1,0:T(8,128)(2,1)S(1)}, u32[]{:S(2)}, u32[]{:S(2)}) collective-permute-start(bf16[48,4224]{1,0:T(8,128)(2,1)S(1)} %get-tuple-element.233), channel_id=1, source_target_pairs={{0,64},{64,0},{1,65},{65,1},{2,66},{66,2},{3,67},{67,3},{4,68},{68... | collective-permute-start | bytes 1216520 | tf_op jit(solution)/shard_map/ppermute | solution.py:34
  459.7 4.4 collective-permute-start.55
  464.2 1.7 collective-permute-start.57
  (28 other events, 218.2 us)
Sparse Core Ops, SparseCore 0:
  28.7 112.2 all-gather.2
  143.1 75.3 all-gather.4
  244.7 85.8 reduce-scatter.4
  334.4 109.1 reduce-scatter.2
